TPU v7x, 32 devices: a whole 2x2x4 slice. The times are simulated.
32 devices in a mesh: dp: 8 (over y, x, core), mp: 4 (over z).
Axes of the slice: x: 2, y: 2, z: 4, core: 2. Of those that a mesh axis runs over, the one named last changes fastest.
Arguments:
- pixels: bfloat16 [32, 196, 768], P('dp'), may hold values from -6 to 6
- visible: int32 [32, 196], P('dp'), may hold values from 0 to 1, as said below
- block_master: float32 [4, 1867776], P('mp', 'dp')
- block_first: float32 [4, 1867776], P('mp', 'dp')
- block_second: float32 [4, 1867776], P('mp', 'dp')
- shared_master: float32 [4128768], P(('dp', 'mp'))
- shared_first: float32 [4128768], P(('dp', 'mp'))
- shared_second: float32 [4128768], P(('dp', 'mp'))
- gains_master: float32 [4352], P(('dp', 'mp'))
- gains_first: float32 [4352], P(('dp', 'mp'))
- gains_second: float32 [4352], P(('dp', 'mp'))
Outputs:
- grad_norm: float32 [], replicated
- loss_sum: float32 [], replicated
- masked_count: float32 [], replicated
- block_first_new: float32 [4, 1867776], P('mp', 'dp')
- block_second_new: float32 [4, 1867776], P('mp', 'dp')
- block_new: float32 [4, 1867776], P('mp', 'dp')
- block_half: bfloat16 [4, 1867776], P('mp', 'dp')
- shared_first_new: float32 [4128768], P(('dp', 'mp'))
- shared_second_new: float32 [4128768], P(('dp', 'mp'))
- shared_new: float32 [4128768], P(('dp', 'mp'))
- shared_half: bfloat16 [4128768], P(('dp', 'mp'))
- gains_first_new: float32 [4352], P(('dp', 'mp'))
- gains_second_new: float32 [4352], P(('dp', 'mp'))
- gains_new: float32 [4352], P(('dp', 'mp'))
- gains_half: bfloat16 [4352], P(('dp', 'mp'))
Inputs may be any that keep to these rules, and one draw needn't show every extreme that they name: In each image the visible patches form one run in raster order that may wrap from the last patch to the first, of 40 to 60 patches; some image has exactly 60 and some exactly 40.
All inputs are finite; a program needn't handle non-finite values.
Results may differ from a plain program's by a relative error of at most 0.0035.
Values may be sent and summed in bfloat16 or wider, within the bound.
No kernel may reach another device: no remote copies, remote signals or barrier semaphores. Data moves between devices by JAX's collectives and lax.ppermute only.
A program may use at most 192 MiB of HBM per device.

v0:
```python
from functools import partial
import math

import jax
import jax.numpy as jnp
from jax import lax
from jax.sharding import PartitionSpec as P

D = 768
HEADS = 12
MLP = 3072
DD = 512
DHEADS = 16
DMLP = 2048
PIX = 768
PATCHES = 196
VIS = 64
STEP = 10


low_type = jnp.bfloat16
clip_norm = 0.0002
beta_one = 0.9
beta_two = 0.95
adam_eps = 1e-10
rate_matrix = 0.03
rate_gains = 0.7
weight_decay = 0.1


def forward_dot(left_side, right_side):
    return jnp.dot(left_side, right_side, preferred_element_type=jnp.float32)


def back_dot(left_side, right_side):
    return lax.dot_general(
        left_side,
        right_side,
        (((left_side.ndim - 1,), (1,)), ((), ())),
        preferred_element_type=jnp.float32,
    )


def outer_sum(left_side, right_side):
    left_rows = left_side.reshape(-1, left_side.shape[-1])
    right_rows = right_side.reshape(-1, right_side.shape[-1])
    return lax.dot_general(
        left_rows, right_rows, (((0,), (0,)), ((), ())), preferred_element_type=jnp.float32
    )


def model_sum(partial_term):
    return lax.psum(partial_term.astype(jnp.bfloat16), "mp").astype(jnp.float32)


def keep_sum(partial_term):
    return partial_term


def position_table(places, row_width):
    column = jnp.arange(row_width)
    step_rate = jnp.exp(-(column // 2 * 2).astype(jnp.float32) * (math.log(10000.0) / row_width))
    angle = places.astype(jnp.float32)[..., None] * step_rate
    return jnp.where(column % 2 == 0, jnp.sin(angle), jnp.cos(angle))


def visible_slots(visible):
    slot_rank = jnp.cumsum(visible, 1) - 1
    select = (
        (visible[:, None, :] == 1) & (slot_rank[:, None, :] == jnp.arange(VIS)[None, :, None])
    ).astype(jnp.int32)
    slot_patch = jnp.sum(select * jnp.arange(visible.shape[1])[None, None, :], 2)
    key_valid = jnp.arange(VIS)[None, :] < jnp.sum(visible, 1)[:, None]
    return (select, slot_patch, key_valid)


def cut_pieces(flat_vector, shapes):
    pieces = []
    offset = 0
    for shape in shapes:
        length = math.prod(shape)
        pieces.append(flat_vector[offset : offset + length].reshape(shape))
        offset += length
    return pieces


def norm_forward(residual, gain_vec):
    center = residual - jnp.mean(residual, -1, keepdims=True)
    inverse = lax.rsqrt(jnp.mean(center * center, -1, keepdims=True) + 1e-06)
    normal_hat = center * inverse
    return (normal_hat * gain_vec, normal_hat, inverse)


def norm_backward(gradient, normal_hat, inverse, gain_vec):
    hat_grad = gradient * gain_vec
    residual_grad = inverse * (
        hat_grad
        - jnp.mean(hat_grad, -1, keepdims=True)
        - normal_hat * jnp.mean(hat_grad * normal_hat, -1, keepdims=True)
    )
    return (residual_grad, gradient * normal_hat)


def split_heads(packed, head_count):
    batch_size, length, row_width = packed.shape
    unpacked = packed.reshape(batch_size, length, 3, head_count, row_width // (3 * head_count))
    return (unpacked[:, :, 0], unpacked[:, :, 1], unpacked[:, :, 2])


def scores_of(query_part, key_part, key_valid, scaling):
    raw_scores = (
        jnp.einsum("blhd,bmhd->bhlm", query_part, key_part, preferred_element_type=jnp.float32)
        * scaling
    )
    return jnp.where(key_valid[:, None, None, :], raw_scores, -1e30)


def attend_forward(packed, key_valid, head_count, scaling):
    query_part, key_part, value_part = split_heads(packed, head_count)
    scores = scores_of(query_part, key_part, key_valid, scaling)
    row_top = jnp.max(scores, -1, keepdims=True)
    exponent = jnp.exp(scores - row_top)
    row_total = jnp.sum(exponent, -1, keepdims=True)
    probability = (exponent / row_total).astype(low_type)
    mixed_heads = jnp.einsum(
        "bhlm,bmhd->blhd", probability, value_part, preferred_element_type=jnp.float32
    )
    batch_size, length = (key_valid.shape[0], packed.shape[1])
    return (
        mixed_heads.reshape(batch_size, length, -1).astype(low_type),
        row_top + jnp.log(row_total),
    )


def attend_backward(packed, log_total, key_valid, mixed_grad, head_count, scaling):
    query_part, key_part, value_part = split_heads(packed, head_count)
    batch_size, length, row_width = mixed_grad.shape
    out_grad = mixed_grad.reshape(batch_size, length, head_count, -1)
    probability = jnp.exp(scores_of(query_part, key_part, key_valid, scaling) - log_total)
    value_grad = jnp.einsum(
        "bhlm,blhd->bmhd",
        probability.astype(low_type),
        out_grad,
        preferred_element_type=jnp.float32,
    )
    prob_grad = jnp.einsum(
        "blhd,bmhd->bhlm", out_grad, value_part, preferred_element_type=jnp.float32
    )
    score_grad = (
        probability * (prob_grad - jnp.sum(probability * prob_grad, -1, keepdims=True))
    ).astype(low_type)
    query_grad = (
        jnp.einsum("bhlm,bmhd->blhd", score_grad, key_part, preferred_element_type=jnp.float32)
        * scaling
    )
    key_grad = (
        jnp.einsum("bhlm,blhd->bmhd", score_grad, query_part, preferred_element_type=jnp.float32)
        * scaling
    )
    stacked = jnp.stack([query_grad, key_grad, value_grad], 2)
    return stacked.reshape(batch_size, length, -1).astype(low_type)


def block_forward(residual, weights, gain_pair, key_valid, head_count, scaling, total_sum):
    packed_w, out_w, up_w, down_w = weights
    first_norm, first_hat, first_inverse = norm_forward(residual, gain_pair[0])
    normed = first_norm.astype(low_type)
    packed = forward_dot(normed, packed_w).astype(low_type)
    mixed_heads, log_total = attend_forward(packed, key_valid, head_count, scaling)
    middle = residual + total_sum(forward_dot(mixed_heads, out_w))
    second_norm, second_hat, second_inverse = norm_forward(middle, gain_pair[1])
    inner_low = second_norm.astype(low_type)
    raised = forward_dot(inner_low, up_w)
    activated = jax.nn.gelu(raised, approximate=True).astype(low_type)
    result = middle + total_sum(forward_dot(activated, down_w))
    saved_values = (
        normed,
        first_hat,
        first_inverse,
        packed,
        log_total,
        mixed_heads,
        second_hat,
        second_inverse,
        inner_low,
        raised,
        activated,
    )
    return (result, saved_values)


def block_backward(
    gradient, saved_values, weights, gain_pair, key_valid, head_count, scaling, total_sum
):
    (
        normed,
        first_hat,
        first_inverse,
        packed,
        log_total,
        mixed_heads,
        second_hat,
        second_inverse,
        inner_low,
        raised,
        activated,
    ) = saved_values
    packed_w, out_w, up_w, down_w = weights
    grad_low = gradient.astype(low_type)
    down_grad = outer_sum(activated, grad_low)
    act_grad = back_dot(grad_low, down_w)
    unused, gelu_back = jax.vjp(partial(jax.nn.gelu, approximate=True), raised)
    raised_grad = gelu_back(act_grad)[0].astype(low_type)
    up_grad = outer_sum(inner_low, raised_grad)
    inner_grad = total_sum(back_dot(raised_grad, up_w))
    middle_part, second_terms = norm_backward(inner_grad, second_hat, second_inverse, gain_pair[1])
    middle_grad = gradient + middle_part
    middle_low = middle_grad.astype(low_type)
    out_grad = outer_sum(mixed_heads, middle_low)
    mixed_grad = back_dot(middle_low, out_w).astype(low_type)
    packed_grad = attend_backward(packed, log_total, key_valid, mixed_grad, head_count, scaling)
    packed_wgrad = outer_sum(normed, packed_grad)
    normed_grad = total_sum(back_dot(packed_grad, packed_w))
    residual_part, first_terms = norm_backward(normed_grad, first_hat, first_inverse, gain_pair[0])
    return (
        middle_grad + residual_part,
        (packed_wgrad, out_grad, up_grad, down_grad),
        (first_terms, second_terms),
    )


def adamw(gradient, first_old, second_old, master, factor, step_rate, decay_rate):
    gradient = gradient * factor
    first_new = beta_one * first_old + (1 - beta_one) * gradient
    second_new = beta_two * second_old + (1 - beta_two) * gradient * gradient
    first_hat = first_new / (1 - beta_one**STEP)
    second_hat = second_new / (1 - beta_two**STEP)
    master_new = master - step_rate * (
        first_hat / (jnp.sqrt(second_hat) + adam_eps) + decay_rate * master
    )
    return (first_new, second_new, master_new, master_new.astype(jnp.bfloat16))


def on_device(
    pixels,
    visible,
    block_master,
    block_first,
    block_second,
    shared_master,
    shared_first,
    shared_second,
    gains_master,
    gains_first,
    gains_second,
):
    groups = lax.axis_size("mp")
    member = lax.axis_index("mp")
    group_images = pixels.shape[0]
    own_images = group_images // groups
    start_image = member * own_images
    own_rows = own_images * VIS

    def own_part(values):
        return lax.dynamic_slice_in_dim(values, start_image, own_images, 0)

    own_visible = own_part(visible)
    hidden_count = jnp.sum(1 - own_visible).astype(jnp.float32)
    count_total = lax.psum(hidden_count, ("dp", "mp"))
    block_flat = lax.all_gather(block_master.astype(low_type), "dp", axis=1, tiled=True)[0]
    shared_flat, gain_flat = (
        lax.all_gather(shared_master.astype(low_type), ("dp", "mp"), axis=0, tiled=True),
        lax.all_gather(gains_master.astype(low_type), ("dp", "mp"), axis=0, tiled=True),
    )
    model_cols = D // groups
    mlp_cols = MLP // groups
    embed_cols = DD // groups
    enc_packed, enc_out, enc_up, enc_down, enc_latent = cut_pieces(
        block_flat,
        [(D, 3 * model_cols), (model_cols, D), (D, mlp_cols), (mlp_cols, D), (D, embed_cols)],
    )
    enc_weights = (enc_packed, enc_out, enc_up, enc_down)
    patch_w, dec_packed, dec_out, dec_up, dec_down, head_w = cut_pieces(
        shared_flat, [(PIX, D), (DD, 3 * DD), (DD, DD), (DD, DMLP), (DMLP, DD), (DD, PIX)]
    )
    dec_weights = (dec_packed, dec_out, dec_up, dec_down)
    gain_values = cut_pieces(
        gain_flat.astype(jnp.float32), [(D,), (D,), (D,), (DD,), (DD,), (DD,), (DD,)]
    )
    enc_one, enc_two, enc_last, dec_one, dec_two, dec_last, mask_token = gain_values
    enc_scaling = (D // HEADS) ** (-0.5)
    dec_scaling = (DD // DHEADS) ** (-0.5)
    select, slot_patch, key_valid = visible_slots(visible)
    seen_patches = jnp.take_along_axis(pixels, slot_patch[:, :, None], 1)
    residual = forward_dot(seen_patches, patch_w) + position_table(slot_patch, D)
    encoded, enc_saved = block_forward(
        residual,
        enc_weights,
        (enc_one, enc_two),
        key_valid,
        HEADS // groups,
        enc_scaling,
        model_sum,
    )
    final_norm, final_hat, final_inverse = norm_forward(encoded, enc_last)
    final_low = final_norm.astype(low_type)
    latent_rows = forward_dot(final_low, enc_latent).astype(low_type).reshape(-1, embed_cols)
    whole_latent = lax.all_gather(latent_rows, "mp", axis=1, tiled=True)
    own_latent = lax.dynamic_slice_in_dim(whole_latent, member * own_rows, own_rows, 0)
    own_latent = own_latent.reshape(own_images, VIS, DD)
    own_select = own_part(select)
    own_patch = own_part(slot_patch)
    own_valid = own_part(key_valid)
    hidden_mask = (1 - own_visible).astype(jnp.float32)
    placed = jnp.einsum(
        "isp,isd->ipd", own_select.astype(low_type), own_latent, preferred_element_type=jnp.float32
    )
    tokens = placed + hidden_mask[:, :, None] * mask_token + position_table(jnp.arange(PATCHES), DD)
    all_valid = jnp.ones(own_visible.shape, bool)
    decoded, dec_saved = block_forward(
        tokens, dec_weights, (dec_one, dec_two), all_valid, DHEADS, dec_scaling, keep_sum
    )
    top_norm, top_hat, top_inverse = norm_forward(decoded, dec_last)
    top_low = top_norm.astype(low_type)
    predicted = forward_dot(top_low, head_w)
    target = own_part(pixels).astype(jnp.float32)
    center = target - jnp.mean(target, -1, keepdims=True)
    target = center * lax.rsqrt(jnp.mean(center * center, -1, keepdims=True) + 1e-06)
    errors = predicted - target
    loss_local = jnp.sum(hidden_mask * jnp.mean(errors * errors, -1))
    pred_grad = (errors * (hidden_mask[:, :, None] * (2.0 / (PIX * count_total)))).astype(low_type)
    head_grad = outer_sum(top_low, pred_grad)
    decoded_grad, dec_last_terms = norm_backward(
        back_dot(pred_grad, head_w), top_hat, top_inverse, dec_last
    )
    token_grad, dec_grads, dec_terms = block_backward(
        decoded_grad,
        dec_saved,
        dec_weights,
        (dec_one, dec_two),
        all_valid,
        DHEADS,
        dec_scaling,
        keep_sum,
    )
    mask_grad = jnp.sum(hidden_mask[:, :, None] * token_grad, (0, 1))
    latent_grad = (
        jnp.take_along_axis(token_grad, own_patch[:, :, None], 1) * own_valid[:, :, None]
    ).astype(low_type)

    def own_total(terms):
        return jnp.sum(own_part(terms), (0, 1))

    latent_grad = latent_grad.reshape(own_rows, DD)
    canvas = jnp.zeros((group_images * VIS, DD), low_type)
    canvas = lax.dynamic_update_slice_in_dim(canvas, latent_grad, member * own_rows, 0)
    latent_return = (
        lax.psum_scatter(canvas, "mp", scatter_dimension=1, tiled=True)
        .astype(jnp.float32)
        .astype(low_type)
    )
    latent_return = latent_return.reshape(group_images, VIS, embed_cols)
    latent_wgrad = outer_sum(final_low, latent_return)
    encoded_grad, enc_last_terms = norm_backward(
        model_sum(back_dot(latent_return, enc_latent)), final_hat, final_inverse, enc_last
    )
    enc_last_grad = own_total(enc_last_terms)
    residual_grad, enc_grads, enc_terms = block_backward(
        encoded_grad,
        enc_saved,
        enc_weights,
        (enc_one, enc_two),
        key_valid,
        HEADS // groups,
        enc_scaling,
        model_sum,
    )
    patch_grad = outer_sum(own_part(seen_patches), own_part(residual_grad).astype(low_type))
    pad_length = gain_flat.shape[0] - 3 * D - 4 * DD
    gain_grad = jnp.concatenate(
        [
            own_total(enc_terms[0]),
            own_total(enc_terms[1]),
            enc_last_grad,
            jnp.sum(dec_terms[0], (0, 1)),
            jnp.sum(dec_terms[1], (0, 1)),
            jnp.sum(dec_last_terms, (0, 1)),
            mask_grad,
            jnp.zeros((pad_length,), jnp.float32),
        ]
    )
    block_grad = jnp.concatenate([piece.reshape(-1) for piece in enc_grads + (latent_wgrad,)])[None]
    shared_grad = jnp.concatenate(
        [piece.reshape(-1) for piece in (patch_grad,) + dec_grads + (head_grad,)]
    )
    block_share = lax.psum_scatter(block_grad, "dp", scatter_dimension=1, tiled=True)
    shared_share, gain_share = (
        lax.psum_scatter(shared_grad, ("dp", "mp"), scatter_dimension=0, tiled=True),
        lax.psum_scatter(gain_grad, ("dp", "mp"), scatter_dimension=0, tiled=True),
    )
    squares = (
        jnp.sum(block_share * block_share)
        + jnp.sum(shared_share * shared_share)
        + jnp.sum(gain_share * gain_share)
    )
    square_total, loss_total = lax.psum((squares, loss_local), ("dp", "mp"))
    grad_norm = jnp.sqrt(square_total)
    factor = jnp.minimum(1.0, clip_norm / (grad_norm + 1e-06))
    block_out = adamw(
        block_share, block_first, block_second, block_master, factor, rate_matrix, weight_decay
    )
    shared_out = adamw(
        shared_share, shared_first, shared_second, shared_master, factor, rate_matrix, weight_decay
    )
    gain_out = adamw(gain_share, gains_first, gains_second, gains_master, factor, rate_gains, 0.0)
    return (grad_norm, loss_total, count_total) + block_out + shared_out + gain_out


def solution(mesh):
    return jax.shard_map(
        on_device,
        mesh=mesh,
        in_specs=(
            P("dp", None, None),
            P("dp", None),
            P("mp", "dp"),
            P("mp", "dp"),
            P("mp", "dp"),
            P(("dp", "mp")),
            P(("dp", "mp")),
            P(("dp", "mp")),
            P(("dp", "mp")),
            P(("dp", "mp")),
            P(("dp", "mp")),
        ),
        out_specs=(
            P(),
            P(),
            P(),
            P("mp", "dp"),
            P("mp", "dp"),
            P("mp", "dp"),
            P("mp", "dp"),
            P(("dp", "mp")),
            P(("dp", "mp")),
            P(("dp", "mp")),
            P(("dp", "mp")),
            P(("dp", "mp")),
            P(("dp", "mp")),
            P(("dp", "mp")),
            P(("dp", "mp")),
        ),
        check_vma=False,
    )
```

profile of v0, /device:TPU:0, one launch (start us, length us, event | category | flops | bytes accessed | tf_op | source)
XLA Modules:
  0.0 899.1 jit_solution(10595356656883082616)
XLA Ops:
  7.3 2.6 convert_element_type.267
  12.0 42.4 %psum.58 = f32[]{:T(128)} all-reduce(f32[]{:T(128)S(6)} %convert_element_type.297), channel_id=1, replica_groups=mesh['dp'=8,'mp'=4] {'dp','mp'}, use_global_device_ids=true, to_apply=%region_25.26 | all-reduce | flops 1 | bytes 8 | tf_op jit(solution)/shard_map/psum | solution.py:269
  56.5 2.4 gather_fusion.1
  59.9 41.4 %all-reduce.1 = bf16[4352]{0:T(1024)(128)(2,1)S(1)} all-reduce(bf16[4352]{0:T(1024)(128)(2,1)S(1)} %dynamic-update-slice), channel_id=1, replica_groups=mesh['dp'=8,'mp'=4] {'dp','mp'}, use_global_device_ids=true, to_apply=%add.1 | all-reduce | flops 4352 | bytes 17408
  105.1 15.8 %slice_reduce_fusion.2 = bf16[442368]{0:T(1024)(128)(2,1)S(1)} fusion(bf16[1,1867776]{1,0:T(2,128)(2,1)} %all-gather.5.cloned.1.call-done), kind=kLoop, calls=%fused_computation.19 | loop fusion | bytes 1769472 | tf_op jit(solution)/shard_map/slice | solution.py:82
  121.7 6.1 slice_reduce_fusion.3
  128.1 17.4 %all-gather.3.cloned.1.call-done = bf16[4128768]{0:T(1024)(128)(2,1)} async-done(((bf16[129024]{0:T(1024)(128)(2,1)}), bf16[4128768]{0:T(1024)(128)(2,1)}) %all-gather.3.cloned.1.call-update) | async-done | bytes 8257552 | tf_op jit(solution)/shard_map/all_gather | solution.py:272
  146.8 1.9 reshape.931
  148.7 5.2 fusion.144
  158.4 27.7 %slice_reduce_fusion = (bf16[589824]{0:T(1024)(128)(2,1)}, bf16[589824]{0:T(1024)(128)(2,1)}) fusion(bf16[1,1867776]{1,0:T(2,128)(2,1)} %all-gather.5.cloned.1.call-done), kind=kLoop, calls=%fused_computation.14 | loop fusion | bytes 4718592 | tf_op jit(solution)/shard_map/slice | solution.py:82
  186.1 2.6 reshape.934
  188.7 3.8 reshape.935
  192.4 2.1 slice_reduce_fusion.4
  197.7 1.4 convolution_convert_fusion.4
  199.1 4.6 fusion.141
  203.7 2.8 slice.205
  206.4 3.3 slice.171
  211.1 4.2 slice.179
  215.3 4.4 slice.181
  219.8 1.6 slice.184
  222.4 13.0 %all-reduce.16.cloned.1.call-done = bf16[4,64,768]{2,1,0:T(8,128)(2,1)} async-done(((bf16[4,64,768]{2,1,0:T(8,128)(2,1)}), bf16[4,64,768]{2,1,0:T(8,128)(2,1)}) %all-reduce.16.cloned.1.call-update) | async-done | bytes 393232 | tf_op jit(solution)/shard_map/psum | solution.py:53
  239.2 13.3 %all_gather.15 = bf16[256,512]{1,0:T(8,128)(2,1)S(1)} all-gather(bf16[256,128]{1,0:T(8,128)(2,1)S(1)} %bitcast.242), channel_id=1, replica_groups=mesh['dp'=8,'mp'=4] {'mp'}, dimensions={1}, use_global_device_ids=true | all-gather | bytes 327680 | tf_op jit(solution)/shard_map/all_gather | solution.py:308
  252.6 1.7 fusion.146
  256.8 1.7 multiply_reduce_fusion.1
  259.1 1.9 fusion.19
  267.7 1.5 fusion.11
  269.2 1.4 multiply_reduce_fusion.15
  273.8 2.0 multiply_reduce_fusion
  283.5 1.9 fusion.132
  285.4 1.9 reshape.905
  287.3 1.4 convolution_bitcast_fusion.6
  290.0 2.8 convolution_bitcast_fusion.1
  292.8 8.9 reduce-scatter.5.cloned.1.call-done
  304.6 2.9 copy.189
  307.6 3.0 copy.190
  312.5 27.5 %all-reduce.18.cloned.1.call-done = bf16[4,64,768]{2,1,0:T(8,128)(2,1)} async-done(((bf16[4,64,768]{2,1,0:T(8,128)(2,1)}), bf16[4,64,768]{2,1,0:T(8,128)(2,1)}) %all-reduce.18.cloned.1.call-update) | async-done | bytes 393232 | tf_op jit(solution)/shard_map/psum | solution.py:53
  345.5 1.9 convolution_bitcast_fusion.4
  347.4 3.3 reshape.898
  350.7 2.1 convolution_bitcast_fusion.3
  352.9 3.3 reshape.899
  356.2 25.5 %all-reduce.20.cloned.1.call-done = bf16[4,64,768]{2,1,0:T(8,128)(2,1)} async-done(((bf16[4,64,768]{2,1,0:T(8,128)(2,1)}), bf16[4,64,768]{2,1,0:T(8,128)(2,1)}) %all-reduce.20.cloned.1.call-update) | async-done | bytes 393232 | tf_op jit(solution)/shard_map/psum | solution.py:53
  383.1 1.5 multiply_add_fusion.1
  389.3 1.3 copy.148
  390.7 1.4 convolution_convert_fusion.1
  392.1 2.1 convolution_bitcast_fusion.5
  394.4 3.0 reshape.896
  397.4 3.0 constant_dynamic-update-slice_fusion.2
  401.2 1.5 constant_dynamic-update-slice_fusion
  403.7 1.6 constant_dynamic-update-slice_fusion.5
  406.5 24.6 %all-reduce.22.cloned.1.call-done = bf16[4,64,768]{2,1,0:T(8,128)(2,1)} async-done(((bf16[4,64,768]{2,1,0:T(8,128)(2,1)}), bf16[4,64,768]{2,1,0:T(8,128)(2,1)}) %all-reduce.22.cloned.1.call-update) | async-done | bytes 393232 | tf_op jit(solution)/shard_map/psum | solution.py:53
  432.4 3.0 fusion.80
  435.4 3.2 reshape.904
  438.7 4.1 constant_dynamic-update-slice_fusion.3
  442.8 1.9 constant_dynamic-update-slice_fusion.1
  447.0 2.4 constant_dynamic-update-slice_fusion.9
  450.7 2.3 constant_dynamic-update-slice_fusion.8
  459.1 40.8 %all-reduce.4 = f32[4352]{0:T(1024)S(1)} all-reduce(f32[4352]{0:T(1024)S(1)} %constant_dynamic-update-slice_fusion.11), channel_id=5, replica_groups=mesh['dp'=8,'mp'=4] {'dp','mp'}, use_global_device_ids=true, to_apply=%region_55.56.clone | all-reduce | flops 4352 | bytes 34816
  500.6 51.3 %all-reduce.24.cloned.1.call-done = f32[1,1867776]{1,0:T(1,128)} async-done(((f32[1,1867776]{1,0:T(1,128)}), f32[1,1867776]{1,0:T(1,128)}) %all-reduce.24.cloned.1.call-update) | async-done | bytes 7471120
  551.9 3.6 multiply_reduce_fusion.2
  555.5 277.8 %all-reduce.26.cloned.1.call-done = f32[4128768]{0:T(1024)} async-done(((f32[4128768]{0:T(1024)}), f32[4128768]{0:T(1024)}) %all-reduce.26.cloned.1.call-update) | async-done | bytes 16515088
  833.2 1.8 multiply_reduce_fusion.12
  837.0 40.6 %all-reduce.5 = (f32[]{:T(128)}, f32[]{:T(128)}) all-reduce(f32[]{:T(128)S(6)} %add.339, f32[]{:T(128)} %multiply_reduce_fusion.27), channel_id=1, replica_groups=mesh['dp'=8,'mp'=4] {'dp','mp'}, use_global_device_ids=true, to_apply=%region_57.58 | all-reduce | flops 2 | bytes 16 | tf_op jit(solution)/shard_map/psum | solution.py:406
  879.0 2.9 fusion.136
  881.9 9.0 %fusion.138 = (bf16[1,233472]{1,0:T(2,128)(2,1)}, f32[1,233472]{1,0:T(1,128)}, f32[1,233472]{1,0:T(1,128)}, f32[1,233472]{1,0:T(1,128)}) fusion(f32[1,233472]{1,0:T(1,128)S(1)} %copy-done.49, f32[]{:T(128)S(6)} %min.3, f32[1,1867776]{1,0:T(1,128)} %all-reduce.24.cloned.1.call-done, u32[]{:T(128)S(6)} %multiply.179, f32[1,233472]{1,0:T(1,128)} %param.15, ...), kind=kLoop, calls=%fused_computation.335 | loop fusion | flops 3969024 | bytes 7004168 | tf_op jit(solution)/shard_map/convert_element_type | solution.py:241
  (462 shorter events, 75.3 us)
Async XLA Ops:
  7.2 49.3 %copy-start = (bf16[4,196,768]{2,0,1:T(4,128)(2,1)S(1)}, bf16[4,196,768]{2,0,1:T(4,128)(2,1)}, u32[]{:S(2)}) copy-start(bf16[4,196,768]{2,0,1:T(4,128)(2,1)} %param.11) | copy-start | bytes 3612676
  7.2 49.3 %copy-start.128 = (f32[136]{0:T(256)S(1)}, f32[136]{0:T(256)}, u32[]{:S(2)}) copy-start(f32[136]{0:T(256)} %param.19) | copy-start | bytes 1636
  7.2 97.9 %all-gather.5.cloned.1.call-start = ((), (), s32[]{:S(2)}) async-start(), calls=%async_computation.2 | async-start | bytes 8404992 | tf_op jit(solution)/shard_map/all_gather | solution.py:270
  9.9 135.7 %all-gather.3.cloned.1.call-start = ((), (), s32[]{:S(2)}) async-start(), calls=%async_computation.1 | async-start | bytes 8515584 | tf_op jit(solution)/shard_map/all_gather | solution.py:272
  10.7 183.9 %all-reduce.14.cloned.1.call-start = ((), (), s32[]{:S(2)}) async-start(), calls=%async_computation.3 | async-start | bytes 786432 | tf_op jit(solution)/shard_map/psum | solution.py:53
  11.4 241.2 %copy-start.122 = (f32[1,196]{1,0:T(1,128)}, f32[1,196]{1,0:T(1,128)S(1)}, u32[]{:S(2)}) copy-start(f32[1,196]{1,0:T(1,128)S(1)} %get-tuple-element.63) | copy-start | bytes 2356
  104.8 161.7 %copy-start.120 = (f32[196]{0:T(256)}, f32[196]{0:T(256)S(1)}, u32[]{:S(2)}) copy-start(f32[196]{0:T(256)S(1)} %broadcast_multiply_fusion.10) | copy-start | bytes 2356
  104.8 149.8 %copy-start.91 = (f32[512]{0:T(512)}, f32[512]{0:T(512)S(1)}, u32[]{:S(2)}) copy-start(f32[512]{0:T(512)S(1)} %get-tuple-element.57) | copy-start | bytes 6148
  104.8 162.7 %copy-start.106 = (f32[512]{0:T(512)}, f32[512]{0:T(512)S(1)}, u32[]{:S(2)}) copy-start(f32[512]{0:T(512)S(1)} %get-tuple-element.55) | copy-start | bytes 6148
  104.8 165.9 %copy-start.87 = (f32[512]{0:T(512)}, f32[512]{0:T(512)S(1)}, u32[]{:S(2)}) copy-start(f32[512]{0:T(512)S(1)} %get-tuple-element.56) | copy-start | bytes 6148
  104.9 49.4 %copy-start.89 = (f32[768]{0:T(1024)}, f32[768]{0:T(1024)S(1)}, u32[]{:S(2)}) copy-start(f32[768]{0:T(1024)S(1)} %get-tuple-element.61) | copy-start | bytes 9220
  104.9 91.4 %copy-start.85 = (f32[768]{0:T(1024)}, f32[768]{0:T(1024)S(1)}, u32[]{:S(2)}) copy-start(f32[768]{0:T(1024)S(1)} %get-tuple-element.60) | copy-start | bytes 9220
  104.9 133.0 %copy-start.83 = (f32[768]{0:T(1024)}, f32[768]{0:T(1024)S(1)}, u32[]{:S(2)}) copy-start(f32[768]{0:T(1024)S(1)} %get-tuple-element.59) | copy-start | bytes 9220
  105.1 43.6 %copy-start.80 = (bf16[4,64,768]{2,1,0:T(8,128)(2,1)}, bf16[4,64,768]{2,1,0:T(8,128)(2,1)S(1)}, u32[]{:S(2)}) copy-start(bf16[4,64,768]{2,1,0:T(8,128)(2,1)S(1)} %broadcast_select_fusion) | copy-start | bytes 1179652
  121.7 32.6 %copy-start.25 = (bf16[768,576]{1,0:T(8,128)(2,1)}, bf16[768,576]{1,0:T(8,128)(2,1)S(1)}, u32[]{:S(2)}) copy-start(bf16[768,576]{1,0:T(8,128)(2,1)S(1)} %reshape.880) | copy-start | bytes 2654212
  128.1 29.2 %copy-start.57 = (bf16[192,768,1]{1,0,2:T(8,128)(2,1)}, bf16[192,768,1]{1,0,2:T(8,128)(2,1)S(1)}, u32[]{:S(2)}) copy-start(bf16[192,768,1]{1,0,2:T(8,128)(2,1)S(1)} %reshape.933) | copy-start | bytes 884740
  153.8 40.8 %copy-start.15 = (f32[4,64,768]{2,1,0:T(8,128)}, f32[4,64,768]{2,1,0:T(8,128)S(1)}, u32[]{:S(2)}) copy-start(f32[4,64,768]{2,1,0:T(8,128)S(1)} %get-tuple-element.65) | copy-start | bytes 2359300
  154.1 67.2 %copy-start.114 = (f32[4,64]{1,0:T(4,128)}, f32[4,64]{1,0:T(4,128)S(1)}, u32[]{:S(2)}) copy-start(f32[4,64]{1,0:T(4,128)S(1)} %add_rsqrt_fusion.2) | copy-start | bytes 3076
  157.2 28.8 %copy-start.75 = (bf16[4,3,64,64]{3,2,1,0:T(8,128)(2,1)}, bf16[4,3,64,64]{3,2,1,0:T(8,128)(2,1)S(1)}, u32[]{:S(2)}) copy-start(bf16[4,3,64,64]{3,2,1,0:T(8,128)(2,1)S(1)} %convolution_convert_fusion.8) | copy-start | bytes 294916
  158.3 77.1 %all-reduce.16.cloned.1.call-start = ((), (), s32[]{:S(2)}) async-start(), calls=%async_computation.4 | async-start | bytes 786432 | tf_op jit(solution)/shard_map/psum | solution.py:53
  188.6 7.6 copy-start.19
  194.6 44.4 %copy-start.67 = (bf16[98304]{0:T(1024)(128)(2,1)}, bf16[98304]{0:T(1024)(128)(2,1)S(1)}, u32[]{:S(2)}) copy-start(bf16[98304]{0:T(1024)(128)(2,1)S(1)} %slice_reduce_fusion.4) | copy-start | bytes 589828
  195.8 42.1 %copy-start.2 = (f32[4,64,768]{2,1,0:T(8,128)}, f32[4,64,768]{2,1,0:T(8,128)S(1)}, u32[]{:S(2)}) copy-start(f32[4,64,768]{2,1,0:T(8,128)S(1)} %get-tuple-element.51) | copy-start | bytes 2359300
  199.1 102.6 %reduce-scatter.5.cloned.1.call-start = ((), (), s32[]{:S(2)}) async-start(), calls=%async_computation.8 | async-start | bytes 327680
  209.8 44.8 %copy-start.12 = (bf16[512,1536]{1,0:T(8,128)(2,1)}, bf16[512,1536]{1,0:T(8,128)(2,1)S(1)}, u32[]{:S(2)}) copy-start(bf16[512,1536]{1,0:T(8,128)(2,1)S(1)} %slice.171) | copy-start | bytes 4718596
  215.3 4.4 slice-start.2
  237.9 16.4 %copy-start.104 = (f32[4,64]{1,0:T(4,128)}, f32[4,64]{1,0:T(4,128)S(1)}, u32[]{:S(2)}) copy-start(f32[4,64]{1,0:T(4,128)S(1)} %add_rsqrt_fusion) | copy-start | bytes 3076
  239.0 13.6 %copy-start.52 = (bf16[4,64,768]{2,1,0:T(8,128)(2,1)}, bf16[4,64,768]{2,1,0:T(8,128)(2,1)S(1)}, u32[]{:S(2)}) copy-start(bf16[4,64,768]{2,1,0:T(8,128)(2,1)S(1)} %get-tuple-element.48) | copy-start | bytes 1179652
  261.5 9.2 %copy-start.17 = (f32[196,512]{1,0:T(8,128)}, f32[196,512]{1,0:T(8,128)S(1)}, u32[]{:S(2)}) copy-start(f32[196,512]{1,0:T(8,128)S(1)} %get-tuple-element.73) | copy-start | bytes 1204228
  261.5 9.2 %copy-start.98 = (f32[196]{0:T(256)}, f32[196]{0:T(256)S(1)}, u32[]{:S(2)}) copy-start(f32[196]{0:T(256)S(1)} %broadcast_multiply_fusion.20) | copy-start | bytes 2356
  261.8 8.9 copy-start.112
  283.4 56.6 %all-reduce.18.cloned.1.call-start = ((), (), s32[]{:S(2)}) async-start(), calls=%async_computation.5 | async-start | bytes 786432 | tf_op jit(solution)/shard_map/psum | solution.py:53
  290.0 12.6 %copy-start.68 = (bf16[98304]{0:T(1024)(128)(2,1)S(1)}, bf16[98304]{0:T(1024)(128)(2,1)}, u32[]{:S(2)}) copy-start(bf16[98304]{0:T(1024)(128)(2,1)} %copy-done.67) | copy-start | bytes 589828
  290.0 13.7 %copy-start.18 = (f32[196,512]{1,0:T(8,128)S(1)}, f32[196,512]{1,0:T(8,128)}, u32[]{:S(2)}) copy-start(f32[196,512]{1,0:T(8,128)} %copy-done.17) | copy-start | bytes 1204228
  290.0 13.7 %copy-start.74 = (bf16[196,2048]{1,0:T(8,128)(2,1)S(1)}, bf16[196,2048]{1,0:T(8,128)(2,1)}, u32[]{:S(2)}) copy-start(bf16[196,2048]{1,0:T(8,128)(2,1)} %copy-done.73) | copy-start | bytes 2408452
  290.0 13.7 %copy-start.88 = (f32[512]{0:T(512)S(1)}, f32[512]{0:T(512)}, u32[]{:S(2)}) copy-start(f32[512]{0:T(512)} %copy-done.87) | copy-start | bytes 6148
  290.0 13.7 %copy-start.99 = (f32[196]{0:T(256)S(1)}, f32[196]{0:T(256)}, u32[]{:S(2)}) copy-start(f32[196]{0:T(256)} %copy-done.98) | copy-start | bytes 2356
  290.0 13.7 %copy-start.113 = (f32[196]{0:T(256)S(1)}, f32[196]{0:T(256)}, u32[]{:S(2)}) copy-start(f32[196]{0:T(256)} %copy-done.112) | copy-start | bytes 2356
  303.7 78.1 %all-reduce.20.cloned.1.call-start = ((), (), s32[]{:S(2)}) async-start(), calls=%async_computation.6 | async-start | bytes 786432 | tf_op jit(solution)/shard_map/psum | solution.py:53
  311.2 28.8 %copy-start.11 = (f32[4,64,768]{2,1,0:T(8,128)S(1)}, f32[4,64,768]{2,1,0:T(8,128)}, u32[]{:S(2)}) copy-start(f32[4,64,768]{2,1,0:T(8,128)} %get-tuple-element.49) | copy-start | bytes 2359300
  311.2 28.8 %copy-start.84 = (f32[768]{0:T(1024)S(1)}, f32[768]{0:T(1024)}, u32[]{:S(2)}) copy-start(f32[768]{0:T(1024)} %copy-done.83) | copy-start | bytes 9220
  311.2 30.0 %copy-start.105 = (f32[4,64]{1,0:T(4,128)S(1)}, f32[4,64]{1,0:T(4,128)}, u32[]{:S(2)}) copy-start(f32[4,64]{1,0:T(4,128)} %copy-done.104) | copy-start | bytes 3076
  312.5 30.0 %copy-start.71 = (bf16[768,768,1]{1,0,2:T(8,128)(2,1)S(1)}, bf16[768,768,1]{1,0,2:T(8,128)(2,1)}, u32[]{:S(2)}) copy-start(bf16[768,768,1]{1,0,2:T(8,128)(2,1)} %reshape.935) | copy-start | bytes 3538948
  312.5 30.0 %copy-start.78 = (f32[4,64,768]{2,1,0:T(8,128)S(1)}, f32[4,64,768]{2,1,0:T(8,128)}, u32[]{:S(2)}) copy-start(f32[4,64,768]{2,1,0:T(8,128)} %copy-done.77) | copy-start | bytes 2359300
  345.0 86.0 %all-reduce.22.cloned.1.call-start = ((), (), s32[]{:S(2)}) async-start(), calls=%async_computation.7 | async-start | bytes 786432 | tf_op jit(solution)/shard_map/psum | solution.py:53
  352.8 28.9 %copy-start.3 = (f32[4,64,768]{2,1,0:T(8,128)S(1)}, f32[4,64,768]{2,1,0:T(8,128)}, u32[]{:S(2)}) copy-start(f32[4,64,768]{2,1,0:T(8,128)} %copy-done.2) | copy-start | bytes 2359300
  352.9 28.9 %copy-start.94 = (f32[4,64]{1,0:T(4,128)S(1)}, f32[4,64]{1,0:T(4,128)}, u32[]{:S(2)}) copy-start(f32[4,64]{1,0:T(4,128)} %copy-done.93) | copy-start | bytes 3076
  352.9 28.9 %copy-start.103 = (f32[4,64]{1,0:T(4,128)S(1)}, f32[4,64]{1,0:T(4,128)}, u32[]{:S(2)}) copy-start(f32[4,64]{1,0:T(4,128)} %copy-done.102) | copy-start | bytes 3076
  352.9 30.2 %copy-start.42 = (bf16[4,64,768]{2,1,0:T(8,128)(2,1)S(1)}, bf16[4,64,768]{2,1,0:T(8,128)(2,1)}, u32[]{:S(2)}) copy-start(bf16[4,64,768]{2,1,0:T(8,128)(2,1)} %all-reduce.18.cloned.1.call-done) | copy-start | bytes 1179652
  352.9 30.2 %copy-start.117 = (f32[4,64]{1,0:T(4,128)S(1)}, f32[4,64]{1,0:T(4,128)}, u32[]{:S(2)}) copy-start(f32[4,64]{1,0:T(4,128)} %copy-done.116) | copy-start | bytes 3076
  356.2 28.4 %copy-start.58 = (bf16[192,768,1]{1,0,2:T(8,128)(2,1)S(1)}, bf16[192,768,1]{1,0,2:T(8,128)(2,1)}, u32[]{:S(2)}) copy-start(bf16[192,768,1]{1,0,2:T(8,128)(2,1)} %copy-done.57) | copy-start | bytes 884740
  394.3 157.7 %all-reduce.24.cloned.1.call-start = ((), (), s32[]{:S(2)}) async-start(), calls=%async_computation.9 | async-start | bytes 14942208
  406.4 24.6 %copy-start.16 = (f32[4,64,768]{2,1,0:T(8,128)S(1)}, f32[4,64,768]{2,1,0:T(8,128)}, u32[]{:S(2)}) copy-start(f32[4,64,768]{2,1,0:T(8,128)} %copy-done.15) | copy-start | bytes 2359300
  406.4 24.6 %copy-start.101 = (f32[4,64]{1,0:T(4,128)S(1)}, f32[4,64]{1,0:T(4,128)}, u32[]{:S(2)}) copy-start(f32[4,64]{1,0:T(4,128)} %copy-done.100) | copy-start | bytes 3076
  406.4 24.6 %copy-start.115 = (f32[4,64]{1,0:T(4,128)S(1)}, f32[4,64]{1,0:T(4,128)}, u32[]{:S(2)}) copy-start(f32[4,64]{1,0:T(4,128)} %copy-done.114) | copy-start | bytes 3076
  406.4 26.0 %copy-start.133 = (f32[1,64]{1,0:T(1,128)S(1)}, f32[1,64]{1,0:T(1,128)}, u32[]{:S(2)}) copy-start(f32[1,64]{1,0:T(1,128)} %constant_dynamic-slice_fusion.4) | copy-start | bytes 772
  406.5 426.8 %all-reduce.26.cloned.1.call-start = ((), (), s32[]{:S(2)}) async-start(), calls=%async_computation.10 | async-start | bytes 33030144
  454.4 4.5 copy-start.69
  457.7 420.6 %copy-start.129 = (f32[136]{0:T(256)S(1)}, f32[136]{0:T(256)}, u32[]{:S(2)}) copy-start(f32[136]{0:T(256)} %param.19) | copy-start | bytes 1636
  457.7 420.6 %copy-start.130 = (f32[136]{0:T(256)S(1)}, f32[136]{0:T(256)}, u32[]{:S(2)}) copy-start(f32[136]{0:T(256)} %param.21) | copy-start | bytes 1636
  457.7 420.6 %copy-start.131 = (f32[136]{0:T(256)S(1)}, f32[136]{0:T(256)}, u32[]{:S(2)}) copy-start(f32[136]{0:T(256)} %param.20) | copy-start | bytes 1636
  457.8 421.3 %copy-start.66 = (f32[129024]{0:T(1024)S(1)}, f32[129024]{0:T(1024)}, u32[]{:S(2)}) copy-start(f32[129024]{0:T(1024)} %param.16) | copy-start | bytes 1548292
  555.5 326.4 %copy-start.49 = (f32[1,233472]{1,0:T(1,128)S(1)}, f32[1,233472]{1,0:T(1,128)}, u32[]{:S(2)}) copy-start(f32[1,233472]{1,0:T(1,128)} %param.13) | copy-start | bytes 2801668
  879.0 11.9 %copy-start.1 = (bf16[4,196,768]{2,0,1:T(4,128)(2,1)S(1)}, bf16[4,196,768]{2,0,1:T(4,128)(2,1)}, u32[]{:S(2)}) copy-start(bf16[4,196,768]{2,0,1:T(4,128)(2,1)} %param.11) | copy-start | bytes 3612676
  (86 other events, 190.5 us)
Sparse Core Ops, SparseCore 0:
  10.5 53.9 all-gather.4
  67.9 77.5 all-gather.2
  158.5 35.6 all-reduce.13
  199.2 36.1 all-reduce.15
  283.5 18.0 reduce-scatter.4
  304.6 35.3 all-reduce.17
  345.1 36.5 all-reduce.19
  394.4 36.6 all-reduce.21
  434.4 117.5 all-reduce.23
  558.0 275.1 all-reduce.25
where the time goes:
time: 905 us; the launch traced here: 899 us
  waiting for transfers between devices  446 us (49%)
  blocking collectives  179 us (20%)
  local copies, waits for them, and re-layouts  151 us (17%)
  matrix products  53.4 us (6%)
  other arithmetic  46.3 us (5%)
  between operations  22.4 us (2%)
    unnamed x13, waiting for transfers between devices  338 us
    psum x5, waiting for transfers between devices, model_sum(): return lax.psum(partial_term.astype(jnp.bfloat16), 'mp').astype(jnp.float32)  90.6 us
    unnamed x2, blocking collectives  82.2 us
    slice x20, local copies, waits for them, and re-layouts, cut_pieces(): pieces.append(flat_vector[offset:offset + length].reshape(shape))  77 us
    psum x1, blocking collectives, on_device(): count_total = lax.psum(hidden_count, ('dp', 'mp'))  42.4 us
    unnamed x298, local copies, waits for them, and re-layouts  40.9 us
    psum x1, blocking collectives, on_device(): square_total, loss_total = lax.psum((squares, loss_local), ('dp', 'mp'))  40.6 us
    dot_general x11, matrix products, outer_sum(): lax.dot_general(left_rows, right_rows, (((0,), (0,)), ((), ())), preferre...  18.8 us
  transfers between devices with their start and end apart: 10, of which 8 were waited for; matrix products, arithmetic and copies ran while one was open for 18% of the time, Pallas kernels for 0%

commit v1 on v0

v1 whole, which is shorter than its diff:
```python
from functools import partial
import math

import jax
import jax.numpy as jnp
from jax import lax
from jax.experimental import pallas as pl
from jax.experimental.pallas import tpu as pltpu
from jax.sharding import PartitionSpec as P

D = 768
HEADS = 12
MLP = 3072
DD = 512
DHEADS = 16
DMLP = 2048
PIX = 768
PATCHES = 196
VIS = 64
STEP = 10


low_type = jnp.bfloat16
clip_norm = 0.0002
beta_one = 0.9
beta_two = 0.95
adam_eps = 1e-10
rate_matrix = 0.03
rate_gains = 0.7
weight_decay = 0.1


def forward_dot(left_side, right_side):
    return jnp.dot(left_side, right_side, preferred_element_type=jnp.float32)


def back_dot(left_side, right_side):
    return lax.dot_general(
        left_side,
        right_side,
        (((left_side.ndim - 1,), (1,)), ((), ())),
        preferred_element_type=jnp.float32,
    )


def outer_sum(left_side, right_side):
    left_rows = left_side.reshape(-1, left_side.shape[-1])
    right_rows = right_side.reshape(-1, right_side.shape[-1])
    return lax.dot_general(
        left_rows, right_rows, (((0,), (0,)), ((), ())), preferred_element_type=jnp.float32
    )


def swap(values, axis_name, distance):
    count = lax.axis_size(axis_name)
    return lax.ppermute(values, axis_name, [(place, place ^ distance) for place in range(count)])


def share(values):
    groups = lax.axis_size("mp")
    return jnp.stack([values] + [swap(values, "mp", step) for step in range(1, groups)])


def collect(partial_terms):
    total = partial_terms[0]
    for step in range(1, partial_terms.shape[0]):
        total = total + swap(partial_terms[step].astype(low_type), "mp", step).astype(jnp.float32)
    return total


def pick(values, index, dim):
    return lax.dynamic_index_in_dim(values, index, dim, keepdims=False)


def reorder(values, place):
    return jnp.stack([pick(values, place ^ step, 0) for step in range(values.shape[0])])


def bits_of(count):
    return count.bit_length() - 1


def after(values, token):
    first = token[(0,) * token.ndim].astype(jnp.float32)
    return values + jnp.minimum(jnp.abs(first), 0.0).astype(values.dtype)


def half_cut(values, side, dim):
    return (pick(values, side, dim), pick(values, 1 - side, dim))


def reduce_dp(values):
    width = bits_of(lax.axis_size("dp"))
    place = lax.axis_index("dp")
    rows = values.shape[1]
    shaped = values.reshape((-1, 2) + values.shape[1:])
    kept_whole, sent_whole = half_cut(shaped, place & 1, 1)
    got_whole = swap(sent_whole, "dp", 1)
    higher = tuple(range(3, width))
    halves = []
    first_marks, second_marks = [], []
    for part, order in (((0, rows // 2), (1, 2) + higher), ((rows // 2, rows), (2, 1) + higher)):
        left = list(range(width - 1, 0, -1))
        split = (2,) * (width - 1) + (part[1] - part[0],) + values.shape[2:]
        both = [
            lax.slice_in_dim(piece, part[0], part[1], axis=1).reshape(split)
            for piece in (kept_whole, got_whole)
        ]
        total = None
        for bit in order:
            dim = left.index(bit)
            side = (place >> bit) & 1
            if total is None:
                kept, sent = [
                    one.astype(jnp.float32) + two.astype(jnp.float32)
                    for one, two in zip(half_cut(both[0], side, dim), half_cut(both[1], side, dim))
                ]
            else:
                kept, sent = half_cut(total, side, dim)
            sent = sent.astype(low_type)
            (first_marks if total is None else second_marks).append(sent)
            total = kept + swap(sent, "dp", 1 << bit).astype(jnp.float32)
            left.remove(bit)
        halves.append(total)
    return jnp.concatenate(halves, 0), first_marks, second_marks


def reduce_mp(values):
    member = lax.axis_index("mp")
    total = pick(values, member, 0)
    for step in range(1, values.shape[0]):
        sent = pick(values, member ^ step, 0).astype(low_type)
        total = total + swap(sent, "mp", step).astype(jnp.float32)
    return total


def gather_small(row):
    table = reorder(share(row), lax.axis_index("mp"))[None]
    for bit in range(bits_of(lax.axis_size("dp"))):
        table = jnp.concatenate([table, swap(table, "dp", 1 << bit)], 0)
    return reorder(table, lax.axis_index("dp")).reshape(-1, row.shape[0])


def sum_small(row):
    for bit in range(bits_of(lax.axis_size("dp"))):
        row = row + swap(row, "dp", 1 << bit)
    return jnp.sum(reorder(share(row), lax.axis_index("mp")), 0)


def pair_permute(values, pairs):
    return lax.ppermute(values, ("dp", "mp"), pairs)


def spread_patch(own_rows, tail_count):
    replicas = lax.axis_size("dp")
    groups = lax.axis_size("mp")
    place = lax.axis_index("dp")
    member = lax.axis_index("mp")
    even = (place & 1) == 0
    for bit in range(1, bits_of(replicas)):
        step = 1 << bit
        pairs = [
            (dp * groups + mp, (dp ^ step) * groups + mp)
            for dp in range(step)
            for mp in range(1 if dp & 1 else groups)
        ]
        own_rows = jnp.where(place < step, own_rows, pair_permute(own_rows, pairs))
    rows = [own_rows]
    for step in range(1, groups):
        pairs = [
            (dp * groups + mp, dp * groups + (mp ^ step))
            for dp in range(replicas)
            for mp in range(1 if dp & 1 else groups)
        ]
        rows.append(pair_permute(own_rows, pairs))
    tail = rows[0][:tail_count]
    for step in range(1, groups):
        tail = jnp.where(member == step, rows[step][:tail_count], tail)
    column = jnp.stack(rows)
    column = jnp.where(even, column, lax.ppermute(column, "dp", [(dp, dp + 1) for dp in range(0, replicas, 2)]))
    tail = jnp.where(even, lax.ppermute(tail, "dp", [(dp + 1, dp) for dp in range(0, replicas, 2)]), tail)
    return jnp.concatenate([reorder(column, member).reshape(-1, D), tail], 0), own_rows


def return_patch(gradient, row_count):
    replicas = lax.axis_size("dp")
    groups = lax.axis_size("mp")
    member = lax.axis_index("mp")
    even = (lax.axis_index("dp") & 1) == 0
    rows = lax.dynamic_slice_in_dim(gradient, member * row_count, row_count, 0)
    tail = gradient[groups * row_count :]
    tail = jnp.pad(tail, ((0, row_count - tail.shape[0]), (0, 0)))
    total = jnp.where(even, rows, tail) + swap(jnp.where(even, tail, rows), "dp", 1)
    total_low = total.astype(low_type)
    for dp in range(2, replicas, 2):
        pairs = [(dp * groups + mp, mp) for mp in range(groups)] + [((dp + 1) * groups, groups)]
        total = total + pair_permute(total_low, pairs).astype(jnp.float32)
    return total


def position_table(places, row_width):
    column = jnp.arange(row_width)
    step_rate = jnp.exp(-(column // 2 * 2).astype(jnp.float32) * (math.log(10000.0) / row_width))
    angle = places.astype(jnp.float32)[..., None] * step_rate
    return jnp.where(column % 2 == 0, jnp.sin(angle), jnp.cos(angle))


def visible_slots(visible):
    slot_rank = jnp.cumsum(visible, 1) - 1
    select = (
        (visible[:, None, :] == 1) & (slot_rank[:, None, :] == jnp.arange(VIS)[None, :, None])
    ).astype(jnp.int32)
    slot_patch = jnp.sum(select * jnp.arange(visible.shape[1])[None, None, :], 2)
    key_valid = jnp.arange(VIS)[None, :] < jnp.sum(visible, 1)[:, None]
    return (select, slot_patch, key_valid)


def cut_pieces(flat_vector, shapes):
    pieces = []
    offset = 0
    for shape in shapes:
        length = math.prod(shape)
        pieces.append(flat_vector[offset : offset + length].reshape(shape))
        offset += length
    return pieces


def norm_forward(residual, gain_vec):
    center = residual - jnp.mean(residual, -1, keepdims=True)
    inverse = lax.rsqrt(jnp.mean(center * center, -1, keepdims=True) + 1e-06)
    normal_hat = center * inverse
    return (normal_hat * gain_vec, normal_hat, inverse)


def norm_backward(gradient, normal_hat, inverse, gain_vec):
    hat_grad = gradient * gain_vec
    residual_grad = inverse * (
        hat_grad
        - jnp.mean(hat_grad, -1, keepdims=True)
        - normal_hat * jnp.mean(hat_grad * normal_hat, -1, keepdims=True)
    )
    return (residual_grad, gradient * normal_hat)


def split_heads(packed, head_count):
    batch_size, length, row_width = packed.shape
    unpacked = packed.reshape(batch_size, length, 3, head_count, row_width // (3 * head_count))
    return (unpacked[:, :, 0], unpacked[:, :, 1], unpacked[:, :, 2])


def scores_of(query_part, key_part, key_valid, scaling):
    raw_scores = (
        jnp.einsum("blhd,bmhd->bhlm", query_part, key_part, preferred_element_type=jnp.float32)
        * scaling
    )
    return jnp.where(key_valid[:, None, None, :], raw_scores, -1e30)


def attend_forward(packed, key_valid, head_count, scaling):
    query_part, key_part, value_part = split_heads(packed, head_count)
    scores = scores_of(query_part, key_part, key_valid, scaling)
    row_top = jnp.max(scores, -1, keepdims=True)
    exponent = jnp.exp(scores - row_top)
    row_total = jnp.sum(exponent, -1, keepdims=True)
    probability = (exponent / row_total).astype(low_type)
    mixed_heads = jnp.einsum(
        "bhlm,bmhd->blhd", probability, value_part, preferred_element_type=jnp.float32
    )
    batch_size, length = (key_valid.shape[0], packed.shape[1])
    return (
        mixed_heads.reshape(batch_size, length, -1).astype(low_type),
        row_top + jnp.log(row_total),
    )


def attend_backward(packed, log_total, key_valid, mixed_grad, head_count, scaling):
    query_part, key_part, value_part = split_heads(packed, head_count)
    batch_size, length, row_width = mixed_grad.shape
    out_grad = mixed_grad.reshape(batch_size, length, head_count, -1)
    probability = jnp.exp(scores_of(query_part, key_part, key_valid, scaling) - log_total)
    value_grad = jnp.einsum(
        "bhlm,blhd->bmhd",
        probability.astype(low_type),
        out_grad,
        preferred_element_type=jnp.float32,
    )
    prob_grad = jnp.einsum(
        "blhd,bmhd->bhlm", out_grad, value_part, preferred_element_type=jnp.float32
    )
    score_grad = (
        probability * (prob_grad - jnp.sum(probability * prob_grad, -1, keepdims=True))
    ).astype(low_type)
    query_grad = (
        jnp.einsum("bhlm,bmhd->blhd", score_grad, key_part, preferred_element_type=jnp.float32)
        * scaling
    )
    key_grad = (
        jnp.einsum("bhlm,blhd->bmhd", score_grad, query_part, preferred_element_type=jnp.float32)
        * scaling
    )
    stacked = jnp.stack([query_grad, key_grad, value_grad], 2)
    return stacked.reshape(batch_size, length, -1).astype(low_type)


def cut_rows(rows, shapes):
    pieces = []
    offset = 0
    for shape in shapes:
        length = math.prod(shape) // 128
        pieces.append(rows[offset : offset + length].reshape(shape))
        offset += length
    return pieces


def mlp_backward(
    gradient, grad_low, activated, raised, inner_low, up_w, down_w, total_sum, norm_saved
):
    down_grad = outer_sum(activated, grad_low)
    act_grad = back_dot(grad_low, down_w)
    unused, gelu_back = jax.vjp(partial(jax.nn.gelu, approximate=True), raised)
    raised_grad = gelu_back(act_grad)[0].astype(low_type)
    up_grad = outer_sum(inner_low, raised_grad)
    inner_grad = total_sum(back_dot(raised_grad, up_w))
    normal_hat, inverse, gain_vec = norm_saved
    middle_part, second_terms = norm_backward(inner_grad, normal_hat, inverse, gain_vec)
    return (gradient + middle_part, down_grad, up_grad, second_terms)


def adamw(gradient, first_old, second_old, master, factor, step_rate, decay_rate):
    gradient = gradient * factor
    first_new = beta_one * first_old + (1 - beta_one) * gradient
    second_new = beta_two * second_old + (1 - beta_two) * gradient * gradient
    first_hat = first_new / (1 - beta_one**STEP)
    second_hat = second_new / (1 - beta_two**STEP)
    master_new = master - step_rate * (
        first_hat / (jnp.sqrt(second_hat) + adam_eps) + decay_rate * master
    )
    return (first_new, second_new, master_new, master_new.astype(jnp.bfloat16))


def low_rows(block_lanes, shared_lanes, row_width):
    pieces = row_width // 128

    def kernel(block_ref, shared_ref, block_out, shared_out, rows_out):
        for source, target in ((block_ref, block_out), (shared_ref, rows_out)):
            rows = target.shape[0]
            for piece in range(pieces):
                lanes = slice(piece * 128, (piece + 1) * 128)
                target[:, lanes] = source[pl.ds(piece, rows, stride=pieces), :].astype(low_type)
        shared_out[...] = shared_ref[...].astype(low_type)

    return pl.pallas_call(
        kernel,
        out_shape=(
            jax.ShapeDtypeStruct((block_lanes.shape[0] // pieces, row_width), low_type),
            jax.ShapeDtypeStruct(shared_lanes.shape, low_type),
            jax.ShapeDtypeStruct((shared_lanes.shape[0] // pieces, row_width), low_type),
        ),
        compiler_params=pltpu.CompilerParams(vmem_limit_bytes=32 * 2**20),
    )(block_lanes, shared_lanes)


def adamw_of(gradient, first_old, second_old, master, step_rate, decay_rate):
    first_new = beta_one * first_old + (1 - beta_one) * gradient
    second_new = beta_two * second_old + (1 - beta_two) * gradient * gradient
    first_hat = first_new / (1 - beta_one**STEP)
    second_hat = second_new / (1 - beta_two**STEP)
    master_new = master - step_rate * (
        first_hat / (jnp.sqrt(second_hat) + adam_eps) + decay_rate * master
    )
    return (first_new, second_new, master_new, master_new.astype(low_type))


def update(factor, block_rows, block_state, shared_lanes, shared_state):
    pieces = block_rows.shape[1] // 128

    def kernel(factor_ref, *refs):
        block_grad, shared_grad = refs[0], refs[4]
        scale = factor_ref[0, 0]
        rows = block_grad.shape[0]
        block_in, block_to = refs[1:4], refs[8:12]
        shared_in, shared_to = refs[5:8], refs[12:16]
        for piece in range(pieces):
            spots = pl.ds(piece, rows, stride=pieces)
            gradient = block_grad[:, piece * 128 : (piece + 1) * 128] * scale
            results = adamw_of(
                gradient, *[ref[spots, :] for ref in block_in], rate_matrix, weight_decay
            )
            for ref, result in zip(block_to[:3], results[:3]):
                ref[spots, :] = result
        block_to[3][...] = block_to[2][...].astype(low_type)
        results = adamw_of(
            shared_grad[...] * scale, *[ref[...] for ref in shared_in], rate_matrix, weight_decay
        )
        for ref, result in zip(shared_to, results):
            ref[...] = result

    kinds = (jnp.float32, jnp.float32, jnp.float32, low_type)
    shapes = [block_state[0].shape] * 4 + [shared_state[0].shape] * 4
    results = pl.pallas_call(
        kernel,
        in_specs=[pl.BlockSpec(memory_space=pltpu.SMEM)]
        + [pl.BlockSpec(memory_space=pltpu.VMEM)] * 8,
        out_shape=[jax.ShapeDtypeStruct(shape, kind) for shape, kind in zip(shapes, kinds * 2)],
        compiler_params=pltpu.CompilerParams(vmem_limit_bytes=40 * 2**20),
    )(factor.reshape(1, 1), block_rows, *block_state, shared_lanes, *shared_state)
    return (tuple(results[:4]), tuple(results[4:]))


TOKENS = 208
LANES = 128


def dot_tn(left_side, right_side):
    return lax.dot_general(
        left_side, right_side, (((0,), (0,)), ((), ())), preferred_element_type=jnp.float32
    )


def dot_nt(left_side, right_side):
    return lax.dot_general(
        left_side, right_side, (((1,), (1,)), ((), ())), preferred_element_type=jnp.float32
    )


def gelu_pair(raised):
    rate = math.sqrt(2.0 / math.pi)
    square = raised * raised
    curve = jnp.tanh(rate * (raised + 0.044715 * raised * square))
    half = 0.5 * (1.0 + curve)
    slope = half + 0.5 * raised * (1.0 - curve * curve) * rate * (1.0 + 0.134145 * square)
    return raised * half, slope


def unpack_kernel(lanes_ref, *refs):
    outs, work = refs[:-1], refs[-1]
    start = PIX * D // LANES
    for out in outs:
        depth, pieces = out.shape[0], out.shape[1] // LANES
        step = 64
        span = step * pieces

        def chunk(index, carry, out=out, start=start, pieces=pieces, span=span):
            source = pl.ds(pl.multiple_of(start + index * span, 64), span)
            work[:span, :] = lanes_ref[source, :].astype(jnp.float32)
            rows = pl.ds(pl.multiple_of(index * step, step), step)
            for piece in range(pieces):
                out[rows, piece * LANES : (piece + 1) * LANES] = work[
                    pl.ds(piece, step, stride=pieces), :
                ].astype(low_type)
            return carry

        lax.fori_loop(0, depth // step, chunk, 0)
        start += depth * pieces


def unpack_decoder(lanes):
    shapes = [(DD, 3 * DD), (DD, DD), (DD, DMLP), (DMLP, DD), (DD, PIX)]
    return pl.pallas_call(
        unpack_kernel,
        out_shape=[jax.ShapeDtypeStruct(shape, low_type) for shape in shapes],
        scratch_shapes=[pltpu.VMEM((64 * DMLP // LANES, LANES), jnp.float32)],
        compiler_params=pltpu.CompilerParams(vmem_limit_bytes=48 * 2**20),
        cost_estimate=pl.CostEstimate(
            flops=0, bytes_accessed=4 * math.prod(lanes.shape), transcendentals=0
        ),
    )(lanes)


def decoder_kernel(
    scale_ref,
    latent_ref,
    select_ref,
    mask_ref,
    table_ref,
    small_ref,
    pixels_ref,
    packed_w,
    out_w,
    up_w,
    down_w,
    head_w,
    grad_out,
    latent_out,
    small_out,
    loss_out,
    work,
    packed_ref,
    mixed_ref,
    prob_ref,
    raised_ref,
    activated_ref,
    packed_grad_ref,
):
    scaling = (DD // DHEADS) ** (-0.5)
    width = DD // DHEADS
    per_block = LANES // width
    first_gain, second_gain, last_gain, mask_token = [
        small_ref[row : row + 1, :] for row in range(4)
    ]
    mask = mask_ref[...]
    select = select_ref[...]
    key_valid = lax.broadcasted_iota(jnp.int32, (TOKENS, TOKENS), 1) < PATCHES
    lane_head = lax.broadcasted_iota(jnp.int32, (TOKENS, LANES), 1) // width
    quarter = DMLP // 4

    tokens = forward_dot(select, latent_ref[...]) + mask * mask_token + table_ref[...]
    first_norm, first_hat, first_inverse = norm_forward(tokens, first_gain)
    normed = first_norm.astype(low_type)
    for piece in range(3):
        columns = slice(piece * DD, (piece + 1) * DD)
        packed_ref[:, columns] = forward_dot(normed, packed_w[:, columns]).astype(low_type)
    mixed_ref[...] = jnp.zeros(mixed_ref.shape, jnp.float32)

    def attend(head, carry):
        block = pl.multiple_of(head // per_block * LANES, LANES)
        inside = lane_head == head % per_block
        query = jnp.where(inside, packed_ref[:, pl.ds(block, LANES)], 0)
        key = packed_ref[:, pl.ds(DD + block, LANES)]
        value = packed_ref[:, pl.ds(2 * DD + block, LANES)]
        scores = jnp.where(key_valid, dot_nt(query, key) * scaling, -1e30)
        exponent = jnp.exp(scores - jnp.max(scores, -1, keepdims=True))
        probability = exponent / jnp.sum(exponent, -1, keepdims=True)
        prob_ref[head] = probability
        mixed = forward_dot(probability.astype(low_type), value)
        mixed_ref[:, pl.ds(block, LANES)] += jnp.where(inside, mixed, 0.0)
        return carry

    lax.fori_loop(0, DHEADS, attend, 0)
    mixed_low = mixed_ref[...].astype(low_type)
    middle = tokens + forward_dot(mixed_low, out_w[...])
    second_norm, second_hat, second_inverse = norm_forward(middle, second_gain)
    inner = second_norm.astype(low_type)
    decoded = middle
    for part in range(4):
        columns = slice(part * quarter, (part + 1) * quarter)
        raised = forward_dot(inner, up_w[:, columns])
        activated, slope = gelu_pair(raised)
        raised_ref[:, columns] = slope
        activated = activated.astype(low_type)
        activated_ref[:, columns] = activated
        decoded = decoded + forward_dot(activated, down_w[columns, :])
    top_norm, top_hat, top_inverse = norm_forward(decoded, last_gain)
    top = top_norm.astype(low_type)
    predicted = forward_dot(top, head_w[...])
    target = pixels_ref[...].astype(jnp.float32)
    center = target - jnp.mean(target, -1, keepdims=True)
    target = center * lax.rsqrt(jnp.mean(center * center, -1, keepdims=True) + 1e-06)
    errors = predicted - target
    loss_out[...] = jnp.sum(
        mask * jnp.mean(errors * errors, -1, keepdims=True), axis=0, keepdims=True
    )
    pred_grad = (errors * (mask * scale_ref[0, 0])).astype(low_type)

    starts = [PIX * D // LANES]
    for size in (3 * DD * DD, DD * DD, DD * DMLP, DMLP * DD):
        starts.append(starts[-1] + size // LANES)
    grad_out[: starts[0], :] = jnp.zeros((starts[0], LANES), low_type)

    def put(left_side, right_ref_columns, pieces, base):
        depth = left_side.shape[1]
        for piece, columns in right_ref_columns:
            product = dot_tn(left_side, columns)
            for half in range(columns.shape[1] // LANES):
                work[pl.ds(base + piece + half, depth, stride=pieces), :] = product[
                    :, half * LANES : (half + 1) * LANES
                ]

    def flush(start, size):
        grad_out[start : start + size, :] = work[:size, :].astype(low_type)

    def pairs_of(values):
        return [
            (2 * pair, values[:, 2 * pair * LANES : 2 * (pair + 1) * LANES])
            for pair in range(values.shape[1] // (2 * LANES))
        ]

    put(top, pairs_of(pred_grad), PIX // LANES, 0)
    flush(starts[4], DD * PIX // LANES)
    decoded_grad, last_terms = norm_backward(
        dot_nt(pred_grad, head_w[...]), top_hat, top_inverse, last_gain
    )
    grad_low = decoded_grad.astype(low_type)
    inner_grad = jnp.zeros((TOKENS, DD), jnp.float32)
    for part in range(4):
        columns = slice(part * quarter, (part + 1) * quarter)
        put(activated_ref[:, columns], pairs_of(grad_low), DD // LANES, part * quarter * DD // LANES)
    flush(starts[3], DMLP * DD // LANES)
    for part in range(4):
        columns = slice(part * quarter, (part + 1) * quarter)
        act_grad = dot_nt(grad_low, down_w[columns, :])
        raised_grad = (act_grad * raised_ref[:, columns]).astype(low_type)
        put(inner, pairs_of(raised_grad), DMLP // LANES, part * quarter // LANES)
        inner_grad = inner_grad + dot_nt(raised_grad, up_w[:, columns])
    flush(starts[2], DD * DMLP // LANES)
    middle_part, second_terms = norm_backward(inner_grad, second_hat, second_inverse, second_gain)
    middle_grad = decoded_grad + middle_part
    middle_low = middle_grad.astype(low_type)
    put(mixed_low, pairs_of(middle_low), DD // LANES, 0)
    flush(starts[1], DD * DD // LANES)
    mixed_ref[...] = dot_nt(middle_low, out_w[...])
    packed_grad_ref[...] = jnp.zeros(packed_grad_ref.shape, jnp.float32)

    def attend_back(head, carry):
        block = pl.multiple_of(head // per_block * LANES, LANES)
        inside = lane_head == head % per_block
        out_grad = mixed_ref[:, pl.ds(block, LANES)].astype(low_type)
        query = packed_ref[:, pl.ds(block, LANES)]
        key = packed_ref[:, pl.ds(DD + block, LANES)]
        value = packed_ref[:, pl.ds(2 * DD + block, LANES)]
        probability = prob_ref[head]
        value_grad = dot_tn(probability.astype(low_type), out_grad)
        prob_grad = dot_nt(jnp.where(inside, out_grad, 0), value)
        score_grad = (
            probability * (prob_grad - jnp.sum(probability * prob_grad, -1, keepdims=True))
        ).astype(low_type)
        query_grad = forward_dot(score_grad, key) * scaling
        key_grad = dot_tn(score_grad, query) * scaling
        for piece, values in enumerate((query_grad, key_grad, value_grad)):
            packed_grad_ref[:, pl.ds(piece * DD + block, LANES)] += jnp.where(inside, values, 0.0)
        return carry

    lax.fori_loop(0, DHEADS, attend_back, 0)
    normed_grad = jnp.zeros((TOKENS, DD), jnp.float32)
    for piece in range(3):
        columns = slice(piece * DD, (piece + 1) * DD)
        packed_low = packed_grad_ref[:, columns].astype(low_type)
        put(normed, pairs_of(packed_low), 3 * DD // LANES, piece * DD // LANES)
        normed_grad = normed_grad + dot_nt(packed_low, packed_w[:, columns])
    flush(starts[0], 3 * DD * DD // LANES)
    token_part, first_terms = norm_backward(normed_grad, first_hat, first_inverse, first_gain)
    token_grad = middle_grad + token_part
    latent_out[...] = dot_tn(select, token_grad.astype(low_type)).astype(low_type)
    for row, terms in enumerate((first_terms, second_terms, last_terms, mask * token_grad)):
        small_out[row : row + 1, :] = jnp.sum(terms, axis=0, keepdims=True)


def decode(scale, latent, select, mask, table, small, pixels, weights, lane_rows):
    return pl.pallas_call(
        decoder_kernel,
        in_specs=[pl.BlockSpec(memory_space=pltpu.SMEM)]
        + [pl.BlockSpec(memory_space=pltpu.VMEM)] * 11,
        out_shape=(
            jax.ShapeDtypeStruct((lane_rows, LANES), low_type),
            jax.ShapeDtypeStruct(latent.shape, low_type),
            jax.ShapeDtypeStruct(small.shape, jnp.float32),
            jax.ShapeDtypeStruct((1, 1), jnp.float32),
        ),
        scratch_shapes=[
            pltpu.VMEM((DD * DMLP // LANES, LANES), jnp.float32),
            pltpu.VMEM((TOKENS, 3 * DD), low_type),
            pltpu.VMEM((TOKENS, DD), jnp.float32),
            pltpu.VMEM((DHEADS, TOKENS, TOKENS), jnp.float32),
            pltpu.VMEM((TOKENS, DMLP), jnp.float32),
            pltpu.VMEM((TOKENS, DMLP), low_type),
            pltpu.VMEM((TOKENS, 3 * DD), jnp.float32),
        ],
        compiler_params=pltpu.CompilerParams(vmem_limit_bytes=60 * 2**20),
        cost_estimate=pl.CostEstimate(
            flops=6 * TOKENS * lane_rows * LANES,
            bytes_accessed=4 * lane_rows * LANES,
            transcendentals=TOKENS * (DMLP + DHEADS * TOKENS),
        ),
    )(scale, latent, select, mask, table, small, pixels, *weights)


def on_device(
    pixels,
    visible,
    block_master,
    block_first,
    block_second,
    shared_master,
    shared_first,
    shared_second,
    gains_master,
    gains_first,
    gains_second,
):
    groups = lax.axis_size("mp")
    replicas = lax.axis_size("dp")
    member = lax.axis_index("mp")
    model_cols = D // groups
    mlp_cols = MLP // groups
    embed_cols = DD // groups
    block_rows = block_master.shape[1] // D
    shared_rows = shared_master.shape[0] // 128

    own_pixels = pick(pixels, member, 0)
    own_visible = pick(visible, member, 0)
    hidden_mask = (1 - own_visible).astype(jnp.float32)
    hidden_count = jnp.sum(1 - own_visible).astype(jnp.float32)

    block_lanes = block_master.reshape(-1, 128)
    shared_lanes = shared_master.reshape(-1, 128)
    block_rowed, shared_low, shared_rowed = low_rows(block_lanes, shared_lanes, D)
    block_flat = lax.all_gather(block_rowed, "dp", axis=0, tiled=True)

    patch_size = PIX * D
    head_rows = shared_master.shape[0] // D
    tail_length = patch_size - groups * head_rows * D
    early = 0 < tail_length <= shared_master.shape[0] and groups * head_rows < PIX
    small_length = gains_master.shape[0]
    small_row = jnp.concatenate([lax.reduce_precision(gains_master, 8, 7), hidden_count[None]])
    small_row = jnp.pad(small_row, (0, -small_row.shape[0] % 128))
    if early:
        patch_w, near_rows = spread_patch(shared_rowed, tail_length // D)
        small_row = after(small_row, near_rows)
        shared_low = after(shared_low, near_rows)
    small_table = gather_small(small_row)
    gain_flat = small_table[:, :small_length].reshape(-1)
    count_total = jnp.sum(small_table[:, small_length])
    shared_column = reorder(share(shared_low), member)
    shared_flat = lax.all_gather(shared_column, "dp", axis=0).reshape(-1, 128)

    bounds = [0, 3 * model_cols, model_cols, mlp_cols, mlp_cols, embed_cols]
    bounds = [sum(bounds[: place + 1]) for place in range(len(bounds))]
    enc_packed, enc_out, enc_up, enc_down, enc_latent = [
        block_flat[low:high] for low, high in zip(bounds[:-1], bounds[1:])
    ]
    enc_packed = enc_packed.reshape(D, 3 * model_cols)
    enc_up = enc_up.reshape(D, mlp_cols)
    own_latent_w = enc_latent.reshape(D, embed_cols)
    latent_w = reorder(share(own_latent_w), member)

    dec_weights = unpack_decoder(shared_flat)
    if not early:
        patch_w = shared_flat[: patch_size // 128].reshape(PIX, D)
    enc_one, enc_two, enc_last, dec_one, dec_two, dec_last, mask_token = cut_pieces(
        gain_flat, [(D,), (D,), (D,), (DD,), (DD,), (DD,), (DD,)]
    )
    enc_scaling = (D // HEADS) ** (-0.5)
    enc_heads = HEADS // groups

    near_visible = reorder(visible, member)
    near_pixels = reorder(pixels, member)
    select, slot_patch, key_valid = visible_slots(near_visible)
    chosen = (slot_patch[:, :, None] == jnp.arange(PATCHES)[None, None, :]).astype(low_type)
    seen_patches = jnp.einsum(
        "isp,ipd->isd", chosen, near_pixels, preferred_element_type=jnp.float32
    ).astype(low_type)
    residual = forward_dot(seen_patches, patch_w) + position_table(slot_patch, D)
    first_norm, first_hat, first_inverse = norm_forward(residual, enc_one)
    normed = first_norm.astype(low_type)
    packed = forward_dot(normed, enc_packed).astype(low_type)
    mixed_heads, log_total = attend_forward(packed, key_valid, enc_heads, enc_scaling)
    middle = residual[0] + collect(forward_dot(mixed_heads, enc_out))
    second_norm, second_hat, second_inverse = norm_forward(middle, enc_two)
    inner_low = share(second_norm.astype(low_type))
    raised = forward_dot(inner_low, enc_up)
    activated = jax.nn.gelu(raised, approximate=True).astype(low_type)
    encoded = middle + collect(forward_dot(activated, enc_down))
    final_norm, final_hat, final_inverse = norm_forward(encoded, enc_last)
    final_low = final_norm.astype(low_type)
    latent = jnp.einsum(
        "sd,mde->sme", final_low, latent_w, preferred_element_type=jnp.float32
    ).astype(low_type)
    latent = latent.reshape(VIS, DD)
    final_all = share(final_low)

    pad = ((0, TOKENS - PATCHES), (0, 0))
    shared_grad, latent_grad, dec_small, loss_local = decode(
        (2.0 / (PIX * count_total)).reshape(1, 1),
        latent,
        jnp.pad(select[0].T.astype(low_type), pad),
        jnp.pad(hidden_mask[:, None], pad),
        jnp.pad(position_table(jnp.arange(PATCHES), DD), pad),
        jnp.pad(jnp.stack([dec_one, dec_two, dec_last, mask_token]), ((0, 4), (0, 0))),
        jnp.pad(own_pixels, pad),
        dec_weights,
        shared_flat.shape[0],
    )
    loss_local = loss_local[0, 0]
    shared_grad = shared_grad.reshape(replicas, groups * shared_rows, 128)
    column_share, first_marks, second_marks = reduce_dp(shared_grad)
    shared_share = reduce_mp(column_share.reshape(groups, shared_rows, 128))

    final_grad = jnp.einsum(
        "sme,mde->sd",
        latent_grad.reshape(VIS, groups, embed_cols),
        latent_w,
        preferred_element_type=jnp.float32,
    )
    encoded_grad, enc_last_terms = norm_backward(final_grad, final_hat, final_inverse, enc_last)
    encoded_low = share(encoded_grad.astype(low_type))
    latent_cut = latent_grad.reshape(VIS, groups, embed_cols)
    latent_near = jnp.stack(
        [pick(latent_cut, member, 1)]
        + [swap(pick(latent_cut, member ^ step, 1), "mp", step) for step in range(1, groups)]
    )
    latent_wgrad = outer_sum(final_all, latent_near)
    middle_grad, down_grad, up_grad, enc_two_terms = mlp_backward(
        encoded_grad,
        encoded_low,
        activated,
        raised,
        inner_low,
        enc_up,
        enc_down,
        collect,
        (second_hat, second_inverse, enc_two),
    )
    middle_low = share(after(middle_grad, first_marks[0] + first_marks[1]).astype(low_type))
    out_grad = outer_sum(mixed_heads, middle_low)
    mixed_grad = back_dot(middle_low, enc_out).astype(low_type)
    pack_grad = attend_backward(packed, log_total, key_valid, mixed_grad, enc_heads, enc_scaling)
    packed_grad = outer_sum(normed, pack_grad)
    residual_part, enc_one_terms = norm_backward(
        collect(after(back_dot(pack_grad, enc_packed), second_marks[0] + second_marks[1])), first_hat[0], first_inverse[0], enc_one
    )
    residual_grad = middle_grad + residual_part
    residual_low = residual_grad.astype(low_type)

    pad_length = gain_flat.shape[0] - 3 * D - 4 * DD
    gain_grad = jnp.concatenate(
        [
            jnp.sum(enc_one_terms, 0),
            jnp.sum(enc_two_terms, 0),
            jnp.sum(enc_last_terms, 0),
            dec_small[:4].reshape(-1),
            jnp.zeros((pad_length,), jnp.float32),
        ]
    )
    block_grad = jnp.concatenate(
        [
            piece.astype(low_type).reshape(-1, D)
            for piece in (packed_grad, out_grad, up_grad, down_grad, latent_wgrad)
        ]
    ).reshape(replicas, block_rows, D)
    block_share = reduce_dp(block_grad)[0]
    place = lax.axis_index("dp")
    if early:
        rows = return_patch(outer_sum(seen_patches, share(residual_low)), head_rows)
        owner = (place == 0) | ((place == 1) & (member == 0))
        shared_share = shared_share + jnp.where(owner, rows.reshape(-1, 128), 0.0)
    else:
        patch_rows = outer_sum(seen_patches[0], residual_low).astype(low_type).reshape(-1, 128)
        patch_rows = jnp.pad(patch_rows, ((0, shared_flat.shape[0] - patch_rows.shape[0]), (0, 0)))
        column = reduce_dp(patch_rows.reshape(replicas, groups * shared_rows, 128))[0]
        shared_share = shared_share + reduce_mp(column.reshape(groups, shared_rows, 128))
    gain_total = sum_small(gain_grad.reshape(-1, 128))
    own = lax.axis_index("dp") * groups + member
    gain_share = lax.dynamic_slice_in_dim(gain_total.reshape(-1), own * small_length, small_length)
    squares = (
        jnp.sum(block_share * block_share)
        + jnp.sum(shared_share * shared_share)
        + jnp.sum(gain_share * gain_share)
    )
    sums = sum_small(jnp.stack([squares, loss_local]).reshape(1, 2))
    square_total, loss_total = sums[0, 0], sums[0, 1]
    grad_norm = jnp.sqrt(square_total)
    factor = jnp.minimum(1.0, clip_norm / (grad_norm + 1e-06))
    block_out, shared_out = update(
        factor,
        block_share,
        [block_first.reshape(-1, 128), block_second.reshape(-1, 128), block_lanes],
        shared_share,
        [shared_first.reshape(-1, 128), shared_second.reshape(-1, 128), shared_lanes],
    )
    block_out = tuple(piece.reshape(block_master.shape) for piece in block_out)
    shared_out = tuple(piece.reshape(-1) for piece in shared_out)
    gain_out = adamw(gain_share, gains_first, gains_second, gains_master, factor, rate_gains, 0.0)
    return (grad_norm, loss_total, count_total) + block_out + shared_out + gain_out


def solution(mesh):
    return jax.shard_map(
        on_device,
        mesh=mesh,
        in_specs=(
            P("dp", None, None),
            P("dp", None),
            P("mp", "dp"),
            P("mp", "dp"),
            P("mp", "dp"),
            P(("dp", "mp")),
            P(("dp", "mp")),
            P(("dp", "mp")),
            P(("dp", "mp")),
            P(("dp", "mp")),
            P(("dp", "mp")),
        ),
        out_specs=(
            P(),
            P(),
            P(),
            P("mp", "dp"),
            P("mp", "dp"),
            P("mp", "dp"),
            P("mp", "dp"),
            P(("dp", "mp")),
            P(("dp", "mp")),
            P(("dp", "mp")),
            P(("dp", "mp")),
            P(("dp", "mp")),
            P(("dp", "mp")),
            P(("dp", "mp")),
            P(("dp", "mp")),
        ),
        check_vma=False,
    )
```

time: 905 us -> 460 us (0.51)
  waiting for transfers between devices: 446 us -> 134 us
  blocking collectives: 179 us -> 0 us
  starting transfers between devices: 0.82 us -> 123 us
  local copies, waits for them, and re-layouts: 151 us -> 66.9 us
  Pallas kernels: 0 us -> 47.2 us
  matrix products: 53.4 us -> 25.3 us
  other arithmetic: 46.3 us -> 30.8 us
    unnamed x13 -> x2, waiting for transfers between devices: 338 us -> 0.03 us
    ppermute x0 -> x78, waiting for transfers between devices: none -> 134 us  [the longest x68 103 us: swap(): lax.ppermute(values, axis_name, [(place, place ^ distance) for place in r...]
    ppermute x0 -> x78, starting transfers between devices: none -> 123 us  [the longest x68 99.7 us: swap(): lax.ppermute(values, axis_name, [(place, place ^ distance) for place in r...]
    psum x5 -> x0, waiting for transfers between devices: 90.6 us -> none  [model_sum(): return lax.psum(partial_term.astype(jnp.bfloat16), 'mp').astype(jnp.float32)]
    psum x2 -> x0, blocking collectives: 83 us -> none  [the longest x1 42.4 us: on_device(): count_total = lax.psum(hidden_count, ('dp', 'mp'))]
    unnamed x2 -> x0, blocking collectives: 82.2 us -> none
    slice x20 -> x2, local copies, waits for them, and re-layouts: 77 us -> 0.01 us  [cut_pieces(): pieces.append(flat_vector[offset:offset + length].reshape(shape))]
    pallas_call x0 -> x4, Pallas kernels: none -> 47.2 us  [the longest x1 34.7 us: decode(): pl.pallas_call(decoder_kernel, in_specs=[pl.BlockSpec(memory_space=pltpu....]
  transfers between devices with their start and end apart: 10 -> 80, of which waited for: 8 -> 41; matrix products, arithmetic and copies ran while one was open for 18% -> 19% of each run, Pallas kernels for 0% -> 0%
where the time goes in v1:
time: 460 us; the launch traced here: 452 us
  waiting for transfers between devices  134 us (29%)
  starting transfers between devices  123 us (27%)
  local copies, waits for them, and re-layouts  66.9 us (15%)
  Pallas kernels  47.2 us (10%)
  other arithmetic  30.8 us (7%)
  matrix products  25.3 us (6%)
  between operations  24.5 us (5%)
    ppermute x68, waiting for transfers between devices, swap(): lax.ppermute(values, axis_name, [(place, place ^ distance) for place in r...  103 us
    ppermute x68, starting transfers between devices, swap(): lax.ppermute(values, axis_name, [(place, place ^ distance) for place in r...  99.7 us
    pallas_call x1, Pallas kernels, decode(): pl.pallas_call(decoder_kernel, in_specs=[pl.BlockSpec(memory_space=pltpu....  34.7 us
    ppermute x8, waiting for transfers between devices, pair_permute(): return lax.ppermute(values, ('dp', 'mp'), pairs)  29.1 us
    unnamed x169, local copies, waits for them, and re-layouts  24.7 us
    ppermute x8, starting transfers between devices, pair_permute(): return lax.ppermute(values, ('dp', 'mp'), pairs)  20.1 us
    dot_general x5, matrix products, forward_dot(): return jnp.dot(left_side, right_side, preferred_element_type=jnp.float32)  9.64 us
  transfers between devices with their start and end apart: 80, of which 41 were waited for; matrix products, arithmetic and copies ran while one was open for 19% of the time, Pallas kernels for 0%

profile of v1, /device:TPU:0, one launch (start us, length us, event | category | flops | bytes accessed | tf_op | source)
XLA Modules:
  0.0 451.8 jit_solution(9487306507965808152)
XLA Ops:
  10.4 4.9 %collective-permute-start = (bf16[168,768]{1,0:T(8,128)(2,1)S(1)}, bf16[168,768]{1,0:T(8,128)(2,1)S(1)}, u32[]{:S(2)}, u32[]{:S(2)}) collective-permute-start(bf16[168,768]{1,0:T(8,128)(2,1)S(1)} %get-tuple-element.35), channel_id=1, source_target_pairs={{0,8},{1,9},{2,10},{3,11},{4,12}} | collective-permute-start | bytes 774152 | tf_op jit(solution)/shard_map/ppermute | solution.py:151
  15.3 5.5 %collective-permute-done = bf16[168,768]{1,0:T(8,128)(2,1)S(1)} collective-permute-done((bf16[168,768]{1,0:T(8,128)(2,1)S(1)}, bf16[168,768]{1,0:T(8,128)(2,1)S(1)}, u32[]{:S(2)}, u32[]{:S(2)}) %collective-permute-start) | collective-permute-done | bytes 258080 | tf_op jit(solution)/shard_map/ppermute | solution.py:151
  22.1 9.9 %collective-permute-done.1 = bf16[168,768]{1,0:T(8,128)(2,1)S(1)} collective-permute-done((bf16[168,768]{1,0:T(8,128)(2,1)S(1)}, bf16[168,768]{1,0:T(8,128)(2,1)S(1)}, u32[]{:S(2)}, u32[]{:S(2)}) %collective-permute-start.1) | collective-permute-done | bytes 258080 | tf_op jit(solution)/shard_map/ppermute | solution.py:151
  34.7 3.0 collective-permute-start.27
  37.7 6.1 %collective-permute-done.25 = bf16[1008,128]{1,0:T(8,128)(2,1)S(1)} collective-permute-done((bf16[1008,128]{1,0:T(8,128)(2,1)S(1)}, bf16[1008,128]{1,0:T(8,128)(2,1)S(1)}, u32[]{:S(2)}, u32[]{:S(2)}) %collective-permute-start.25) | collective-permute-done | bytes 258080 | tf_op jit(solution)/shard_map/ppermute | solution.py:56
  43.8 10.6 %collective-permute-done.26 = bf16[1008,128]{1,0:T(8,128)(2,1)S(1)} collective-permute-done((bf16[1008,128]{1,0:T(8,128)(2,1)S(1)}, bf16[1008,128]{1,0:T(8,128)(2,1)S(1)}, u32[]{:S(2)}, u32[]{:S(2)}) %collective-permute-start.26) | collective-permute-done | bytes 258080 | tf_op jit(solution)/shard_map/ppermute | solution.py:56
  57.5 2.5 constant_dynamic-slice_fusion.34
  64.9 4.8 %collective-permute-start.7 = (f32[256]{0:T(256)S(1)}, f32[256]{0:T(256)S(1)}, u32[]{:S(2)}, u32[]{:S(2)}) collective-permute-start(f32[256]{0:T(256)S(1)} %fusion.124), channel_id=1, source_target_pairs={{0,1},{1,0},{2,3},{3,2},{4,5},{5,4},{6,7},{7,6},{8,9},{9,8},{10,11... | collective-permute-start | bytes 3080 | tf_op jit(solution)/shard_map/ppermute | solution.py:56
  69.7 2.4 collective-permute-start.9
  78.0 2.2 collective-permute-done.11
  80.2 2.4 collective-permute-start.12
  85.6 2.1 collective-permute-start.2
  87.7 4.8 %collective-permute-start.3 = (bf16[168,768]{1,0:T(8,128)(2,1)S(1)}, bf16[168,768]{1,0:T(8,128)(2,1)S(1)}, u32[]{:S(2)}, u32[]{:S(2)}) collective-permute-start(bf16[168,768]{1,0:T(8,128)(2,1)S(1)} %broadcast_select_fusion.2), channel_id=1, source_target_pairs={{0,2},{1,3},{2,0},{3,1},{4,6},{8,10},{9,11},{10,8},{11,9},{12,14},... | collective-permute-start | bytes 774152 | tf_op jit(solution)/shard_map/ppermute | solution.py:151
  92.5 3.2 collective-permute-start.4
  96.0 3.9 collective-permute-done.3
  100.0 3.6 collective-permute-done.4
  111.1 3.1 fusion.160
  114.7 2.4 slice.266
  117.1 2.7 reshape.526
  125.0 5.8 %collective-permute-start.13 = (bf16[64,768]{1,0:T(8,128)(2,1)}, bf16[64,768]{1,0:T(8,128)(2,1)}, u32[]{:S(2)}, u32[]{:S(2)}) collective-permute-start(bf16[64,768]{1,0:T(8,128)(2,1)} %get-tuple-element.126), channel_id=1, source_target_pairs={{0,1},{1,0},{2,3},{3,2},{4,5},{5,4},{6,7},{7,6},{8,9},{9,8},{10,11... | collective-permute-start | bytes 294920 | tf_op jit(solution)/shard_map/ppermute | solution.py:56
  130.8 2.0 collective-permute-start.14
  136.5 2.4 collective-permute-start.23
  139.2 3.2 collective-permute-done.15
  149.5 4.4 collective-permute-start.24
  153.9 8.6 %collective-permute-done.17 = bf16[64,768]{1,0:T(8,128)(2,1)S(1)} collective-permute-done((bf16[64,768]{1,0:T(8,128)(2,1)S(1)}, bf16[64,768]{1,0:T(8,128)(2,1)S(1)}, u32[]{:S(2)}, u32[]{:S(2)}) %collective-permute-start.17) | collective-permute-done | bytes 98336 | tf_op jit(solution)/shard_map/ppermute | solution.py:56
  164.3 2.2 fusion.163
  166.6 2.7 collective-permute-start.19
  172.9 6.9 %collective-permute-done.20 = bf16[64,768]{1,0:T(8,128)(2,1)S(1)} collective-permute-done((bf16[64,768]{1,0:T(8,128)(2,1)S(1)}, bf16[64,768]{1,0:T(8,128)(2,1)S(1)}, u32[]{:S(2)}, u32[]{:S(2)}) %collective-permute-start.20) | collective-permute-done | bytes 98336 | tf_op jit(solution)/shard_map/ppermute | solution.py:56
  182.7 8.0 %shard_map.227 = (bf16[512,1536]{1,0:T(8,128)(2,1)S(1)}, bf16[512,512]{1,0:T(8,128)(2,1)S(1)}, bf16[512,2048]{1,0:T(8,128)(2,1)S(1)}, bf16[2048,512]{1,0:T(8,128)(2,1)}, bf16[512,768]{1,0:T(8,128)(2,1)S(1)}) custom-call(bf16[32256,128]{1,0:T(8,128)(2,1)} %bitcast.428), custom_call_target="tpu_custom_call" | custom-call | bytes 16515072 | tf_op jit(solution)/shard_map/pallas_call | solution.py:459
  194.9 34.7 %shard_map.228 = (bf16[32256,128]{1,0:T(8,128)(2,1)}, bf16[64,512]{1,0:T(8,128)(2,1)}, f32[8,512]{1,0:T(8,128)}, f32[1,1]{1,0:T(1,128)}) custom-call(f32[1,1]{1,0:T(1,128)} %bitcast.39.scale_ref, bf16[64,512]{1,0:T(8,128)(2,1)} %bitcast.485, bf16[208,64]{1,0:T(8,128)(2,1)} %pad.33.select_ref, f32[208,1]{1,0:T(8,128)} %pad.34.mask_ref, ...), custom_call_target="tpu_custom_call" | custom-call | flops 5152702464 | bytes 16515072 | tf_op jit(solution)/shard_map/pallas_call | solution.py:639
  229.6 7.4 %dynamic-slice_bitcast_fusion.1 = (bf16[4,4032,128]{2,1,0:T(8,128)(2,1)}, bf16[4,4032,128]{2,1,0:T(8,128)(2,1)}) fusion(bf16[4,2,4032,128]{3,2,1,0:T(8,128)(2,1)} %bitcast.429, s32[]{:T(128)S(6)} %select_n.287, s32[]{:T(128)S(6)} %select_n.289), kind=kLoop, calls=%fused_computation.1 | loop fusion | bytes 16515080 | tf_op jit(solution)/shard_map/jit(dynamic_index_in_dim)/squeeze | solution.py:72
  241.2 2.6 collective-permute-start.29
  246.0 2.0 collective-permute-done.28
  248.0 4.3 collective-permute-done.30
  259.2 2.7 collective-permute-start.39
  261.8 5.4 %collective-permute-done.32 = bf16[64,768]{1,0:T(8,128)(2,1)S(1)} collective-permute-done((bf16[64,768]{1,0:T(8,128)(2,1)S(1)}, bf16[64,768]{1,0:T(8,128)(2,1)S(1)}, u32[]{:S(2)}, u32[]{:S(2)}) %collective-permute-start.32) | collective-permute-done | bytes 98336 | tf_op jit(solution)/shard_map/ppermute | solution.py:56
  267.3 2.0 collective-permute-start.40
  269.3 2.3 collective-permute-start.42
  271.8 2.0 collective-permute-start.43
  273.8 2.5 fusion.154
  281.6 2.1 collective-permute-start.35
  284.2 2.0 collective-permute-start.37
  288.7 2.9 collective-permute-done.36
  291.6 2.1 convolution_convert_fusion.3
  299.1 2.1 copy.218
  301.2 2.7 bitcast_convert_fusion.2
  303.9 2.3 copy.220
  306.1 3.4 reshape.538
  327.0 4.5 collective-permute-done.57
  334.6 2.2 collective-permute-done.67
  338.0 8.6 %collective-permute-done.68 = f32[34,128]{1,0:T(8,128)S(1)} collective-permute-done((f32[34,128]{1,0:T(8,128)S(1)}, f32[34,128]{1,0:T(8,128)S(1)}, u32[]{:S(2)}, u32[]{:S(2)}) %collective-permute-start.68) | collective-permute-done | bytes 17440 | tf_op jit(solution)/shard_map/ppermute | solution.py:56
  358.9 3.2 collective-permute-done.60
  362.9 5.9 %collective-permute-done.52 = bf16[2016,128]{1,0:T(8,128)(2,1)S(1)} collective-permute-done((bf16[2016,128]{1,0:T(8,128)(2,1)S(1)}, bf16[2016,128]{1,0:T(8,128)(2,1)S(1)}, u32[]{:S(2)}, u32[]{:S(2)}) %collective-permute-start.52) | collective-permute-done | bytes 516128 | tf_op jit(solution)/shard_map/ppermute | solution.py:56
  370.0 2.5 collective-permute-start.54
  378.6 2.2 collective-permute-done.63
  382.7 4.0 collective-permute-done.64
  389.9 2.2 multiply_reduce_fusion.2
  392.1 3.7 collective-permute-done.45
  403.3 2.5 collective-permute-done.48
  416.3 2.7 collective-permute-done.74
  421.0 2.5 collective-permute-start.77
  423.5 2.8 collective-permute-done.77
  431.1 3.6 shard_map.229
  434.7 8.2 %copy.282 = bf16[1,1,1824,128]{3,1,2,0:T(2,128)(2,1)} copy(bf16[1,1,1824,128]{3,2,1,0:T(8,128)(2,1)S(1)} %bitcast.427) | data formatting | bytes 933888
  (457 shorter events, 152.4 us)
Async XLA Ops:
  7.2 107.5 %all-gather.4.cloned.1.call-start = ((), (), s32[]{:S(2)}) async-start(), calls=%async_computation | async-start | bytes 4202496 | tf_op jit(solution)/shard_map/all_gather | solution.py:697
  10.4 172.3 %all-gather.6.cloned.1.call-start = ((), (), s32[]{:S(2)}) async-start(), calls=%async_computation.1 | async-start | bytes 9289728 | tf_op jit(solution)/shard_map/all_gather | solution.py:714
  10.4 10.3 %collective-permute-start = (bf16[168,768]{1,0:T(8,128)(2,1)S(1)}, bf16[168,768]{1,0:T(8,128)(2,1)S(1)}, u32[]{:S(2)}, u32[]{:S(2)}) collective-permute-start(bf16[168,768]{1,0:T(8,128)(2,1)S(1)} %get-tuple-element.35), channel_id=1, source_target_pairs={{0,8},{1,9},{2,10},{3,11},{4,12}} | collective-permute-start | bytes 774152 | tf_op jit(solution)/shard_map/ppermute | solution.py:151
  20.8 11.2 %collective-permute-start.1 = (bf16[168,768]{1,0:T(8,128)(2,1)S(1)}, bf16[168,768]{1,0:T(8,128)(2,1)S(1)}, u32[]{:S(2)}, u32[]{:S(2)}) collective-permute-start(bf16[168,768]{1,0:T(8,128)(2,1)S(1)} %broadcast_select_fusion.1), channel_id=1, source_target_pairs={{0,16},{1,17},{2,18},{3,19},{4,20},{8,24},{9,25},{10,26},{11,27},{... | collective-permute-start | bytes 774152 | tf_op jit(solution)/shard_map/ppermute | solution.py:151
  33.3 10.6 %collective-permute-start.25 = (bf16[1008,128]{1,0:T(8,128)(2,1)S(1)}, bf16[1008,128]{1,0:T(8,128)(2,1)S(1)}, u32[]{:S(2)}, u32[]{:S(2)}) collective-permute-start(bf16[1008,128]{1,0:T(8,128)(2,1)S(1)} %broadcast_add_fusion), channel_id=1, source_target_pairs={{0,1},{1,0},{2,3},{3,2},{4,5},{5,4},{6,7},{7,6},{8,9},{9,8},{10,11... | collective-permute-start | bytes 774152 | tf_op jit(solution)/shard_map/ppermute | solution.py:56
  33.3 21.1 %collective-permute-start.26 = (bf16[1008,128]{1,0:T(8,128)(2,1)S(1)}, bf16[1008,128]{1,0:T(8,128)(2,1)S(1)}, u32[]{:S(2)}, u32[]{:S(2)}) collective-permute-start(bf16[1008,128]{1,0:T(8,128)(2,1)S(1)} %broadcast_add_fusion), channel_id=1, source_target_pairs={{0,2},{1,3},{2,0},{3,1},{4,6},{5,7},{6,4},{7,5},{8,10},{9,11},{10,... | collective-permute-start | bytes 774152 | tf_op jit(solution)/shard_map/ppermute | solution.py:56
  34.7 19.7 %collective-permute-start.27 = (bf16[1008,128]{1,0:T(8,128)(2,1)S(1)}, bf16[1008,128]{1,0:T(8,128)(2,1)S(1)}, u32[]{:S(2)}, u32[]{:S(2)}) collective-permute-start(bf16[1008,128]{1,0:T(8,128)(2,1)S(1)} %broadcast_add_fusion), channel_id=1, source_target_pairs={{0,3},{1,2},{2,1},{3,0},{4,7},{5,6},{6,5},{7,4},{8,11},{9,10},{10,... | collective-permute-start | bytes 774152 | tf_op jit(solution)/shard_map/ppermute | solution.py:56
  64.9 7.4 %collective-permute-start.7 = (f32[256]{0:T(256)S(1)}, f32[256]{0:T(256)S(1)}, u32[]{:S(2)}, u32[]{:S(2)}) collective-permute-start(f32[256]{0:T(256)S(1)} %fusion.124), channel_id=1, source_target_pairs={{0,1},{1,0},{2,3},{3,2},{4,5},{5,4},{6,7},{7,6},{8,9},{9,8},{10,11... | collective-permute-start | bytes 3080 | tf_op jit(solution)/shard_map/ppermute | solution.py:56
  80.2 15.6 %collective-permute-start.12 = (f32[4,4,256]{2,1,0:T(4,128)S(1)}, f32[4,4,256]{2,1,0:T(4,128)S(1)}, u32[]{:S(2)}, u32[]{:S(2)}) collective-permute-start(f32[4,4,256]{2,1,0:T(4,128)S(1)} %pad_maximum_fusion.21), channel_id=1, source_target_pairs={{0,16},{4,20},{8,24},{12,28},{16,0},{20,4},{24,8},{28,12},{1,17},{... | collective-permute-start | bytes 49160 | tf_op jit(solution)/shard_map/ppermute | solution.py:56
  85.6 10.4 %collective-permute-start.2 = (bf16[168,768]{1,0:T(8,128)(2,1)S(1)}, bf16[168,768]{1,0:T(8,128)(2,1)S(1)}, u32[]{:S(2)}, u32[]{:S(2)}) collective-permute-start(bf16[168,768]{1,0:T(8,128)(2,1)S(1)} %broadcast_select_fusion.2), channel_id=1, source_target_pairs={{0,1},{1,0},{2,3},{3,2},{4,5},{8,9},{9,8},{10,11},{11,10},{12,13},... | collective-permute-start | bytes 774152 | tf_op jit(solution)/shard_map/ppermute | solution.py:151
  87.7 12.2 %collective-permute-start.3 = (bf16[168,768]{1,0:T(8,128)(2,1)S(1)}, bf16[168,768]{1,0:T(8,128)(2,1)S(1)}, u32[]{:S(2)}, u32[]{:S(2)}) collective-permute-start(bf16[168,768]{1,0:T(8,128)(2,1)S(1)} %broadcast_select_fusion.2), channel_id=1, source_target_pairs={{0,2},{1,3},{2,0},{3,1},{4,6},{8,10},{9,11},{10,8},{11,9},{12,14},... | collective-permute-start | bytes 774152 | tf_op jit(solution)/shard_map/ppermute | solution.py:151
  92.5 11.1 %collective-permute-start.4 = (bf16[168,768]{1,0:T(8,128)(2,1)S(1)}, bf16[168,768]{1,0:T(8,128)(2,1)S(1)}, u32[]{:S(2)}, u32[]{:S(2)}) collective-permute-start(bf16[168,768]{1,0:T(8,128)(2,1)S(1)} %broadcast_select_fusion.2), channel_id=1, source_target_pairs={{0,3},{1,2},{2,1},{3,0},{4,7},{8,11},{9,10},{10,9},{11,8},{12,15},... | collective-permute-start | bytes 774152 | tf_op jit(solution)/shard_map/ppermute | solution.py:151
  103.7 6.2 %collective-permute-start.5 = (bf16[4,168,768]{2,1,0:T(8,128)(2,1)S(1)}, bf16[4,168,768]{2,1,0:T(8,128)(2,1)S(1)}, u32[]{:S(2)}, u32[]{:S(2)}) collective-permute-start(bf16[4,168,768]{2,1,0:T(8,128)(2,1)S(1)} %pad_maximum_fusion.1), channel_id=1, source_target_pairs={{0,4},{8,12},{16,20},{24,28},{1,5},{9,13},{17,21},{25,29},{2,6},{1... | collective-permute-start | bytes 3096584 | tf_op jit(solution)/shard_map/ppermute | solution.py:180
  125.0 14.2 %collective-permute-start.13 = (bf16[64,768]{1,0:T(8,128)(2,1)}, bf16[64,768]{1,0:T(8,128)(2,1)}, u32[]{:S(2)}, u32[]{:S(2)}) collective-permute-start(bf16[64,768]{1,0:T(8,128)(2,1)} %get-tuple-element.126), channel_id=1, source_target_pairs={{0,1},{1,0},{2,3},{3,2},{4,5},{5,4},{6,7},{7,6},{8,9},{9,8},{10,11... | collective-permute-start | bytes 294920 | tf_op jit(solution)/shard_map/ppermute | solution.py:56
  130.8 8.4 %collective-permute-start.14 = (bf16[64,768]{1,0:T(8,128)(2,1)}, bf16[64,768]{1,0:T(8,128)(2,1)}, u32[]{:S(2)}, u32[]{:S(2)}) collective-permute-start(bf16[64,768]{1,0:T(8,128)(2,1)} %get-tuple-element.128), channel_id=1, source_target_pairs={{0,2},{1,3},{2,0},{3,1},{4,6},{5,7},{6,4},{7,5},{8,10},{9,11},{10,... | collective-permute-start | bytes 294920 | tf_op jit(solution)/shard_map/ppermute | solution.py:56
  132.7 9.6 %collective-permute-start.15 = (bf16[64,768]{1,0:T(8,128)(2,1)}, bf16[64,768]{1,0:T(8,128)(2,1)}, u32[]{:S(2)}, u32[]{:S(2)}) collective-permute-start(bf16[64,768]{1,0:T(8,128)(2,1)} %get-tuple-element.127), channel_id=1, source_target_pairs={{0,3},{1,2},{2,1},{3,0},{4,7},{5,6},{6,5},{7,4},{8,11},{9,10},{10,... | collective-permute-start | bytes 294920 | tf_op jit(solution)/shard_map/ppermute | solution.py:56
  135.9 34.6 %collective-permute-start.22 = (bf16[768,128]{1,0:T(8,128)(2,1)S(1)}, bf16[768,128]{1,0:T(8,128)(2,1)S(1)}, u32[]{:S(2)}, u32[]{:S(2)}) collective-permute-start(bf16[768,128]{1,0:T(8,128)(2,1)S(1)} %reshape.529), channel_id=1, source_target_pairs={{0,1},{1,0},{2,3},{3,2},{4,5},{5,4},{6,7},{7,6},{8,9},{9,8},{10,11... | collective-permute-start | bytes 589832 | tf_op jit(solution)/shard_map/ppermute | solution.py:56
  136.5 35.4 %collective-permute-start.23 = (bf16[768,128]{1,0:T(8,128)(2,1)S(1)}, bf16[768,128]{1,0:T(8,128)(2,1)S(1)}, u32[]{:S(2)}, u32[]{:S(2)}) collective-permute-start(bf16[768,128]{1,0:T(8,128)(2,1)S(1)} %reshape.529), channel_id=1, source_target_pairs={{0,2},{1,3},{2,0},{3,1},{4,6},{5,7},{6,4},{7,5},{8,10},{9,11},{10,... | collective-permute-start | bytes 589832 | tf_op jit(solution)/shard_map/ppermute | solution.py:56
  143.8 5.7 %collective-permute-start.16 = (bf16[64,768]{1,0:T(8,128)(2,1)S(1)}, bf16[64,768]{1,0:T(8,128)(2,1)S(1)}, u32[]{:S(2)}, u32[]{:S(2)}) collective-permute-start(bf16[64,768]{1,0:T(8,128)(2,1)S(1)} %multiply_convert_fusion.4), channel_id=1, source_target_pairs={{0,1},{1,0},{2,3},{3,2},{4,5},{5,4},{6,7},{7,6},{8,9},{9,8},{10,11... | collective-permute-start | bytes 294920 | tf_op jit(solution)/shard_map/ppermute | solution.py:56
  145.7 16.8 %collective-permute-start.17 = (bf16[64,768]{1,0:T(8,128)(2,1)S(1)}, bf16[64,768]{1,0:T(8,128)(2,1)S(1)}, u32[]{:S(2)}, u32[]{:S(2)}) collective-permute-start(bf16[64,768]{1,0:T(8,128)(2,1)S(1)} %multiply_convert_fusion.4), channel_id=1, source_target_pairs={{0,2},{1,3},{2,0},{3,1},{4,6},{5,7},{6,4},{7,5},{8,10},{9,11},{10,... | collective-permute-start | bytes 294920 | tf_op jit(solution)/shard_map/ppermute | solution.py:56
  147.7 14.8 %collective-permute-start.18 = (bf16[64,768]{1,0:T(8,128)(2,1)S(1)}, bf16[64,768]{1,0:T(8,128)(2,1)S(1)}, u32[]{:S(2)}, u32[]{:S(2)}) collective-permute-start(bf16[64,768]{1,0:T(8,128)(2,1)S(1)} %multiply_convert_fusion.4), channel_id=1, source_target_pairs={{0,3},{1,2},{2,1},{3,0},{4,7},{5,6},{6,5},{7,4},{8,11},{9,10},{10,... | collective-permute-start | bytes 294920 | tf_op jit(solution)/shard_map/ppermute | solution.py:56
  149.5 22.4 %collective-permute-start.24 = (bf16[768,128]{1,0:T(8,128)(2,1)S(1)}, bf16[768,128]{1,0:T(8,128)(2,1)S(1)}, u32[]{:S(2)}, u32[]{:S(2)}) collective-permute-start(bf16[768,128]{1,0:T(8,128)(2,1)S(1)} %reshape.529), channel_id=1, source_target_pairs={{0,3},{1,2},{2,1},{3,0},{4,7},{5,6},{6,5},{7,4},{8,11},{9,10},{10,... | collective-permute-start | bytes 589832 | tf_op jit(solution)/shard_map/ppermute | solution.py:56
  166.6 6.3 %collective-permute-start.19 = (bf16[64,768]{1,0:T(8,128)(2,1)S(1)}, bf16[64,768]{1,0:T(8,128)(2,1)S(1)}, u32[]{:S(2)}, u32[]{:S(2)}) collective-permute-start(bf16[64,768]{1,0:T(8,128)(2,1)S(1)} %get-tuple-element.123), channel_id=1, source_target_pairs={{0,1},{1,0},{2,3},{3,2},{4,5},{5,4},{6,7},{7,6},{8,9},{9,8},{10,11... | collective-permute-start | bytes 294920 | tf_op jit(solution)/shard_map/ppermute | solution.py:56
  169.3 10.6 %collective-permute-start.20 = (bf16[64,768]{1,0:T(8,128)(2,1)S(1)}, bf16[64,768]{1,0:T(8,128)(2,1)S(1)}, u32[]{:S(2)}, u32[]{:S(2)}) collective-permute-start(bf16[64,768]{1,0:T(8,128)(2,1)S(1)} %get-tuple-element.125), channel_id=1, source_target_pairs={{0,2},{1,3},{2,0},{3,1},{4,6},{5,7},{6,4},{7,5},{8,10},{9,11},{10,... | collective-permute-start | bytes 294920 | tf_op jit(solution)/shard_map/ppermute | solution.py:56
  170.5 9.3 %collective-permute-start.21 = (bf16[64,768]{1,0:T(8,128)(2,1)S(1)}, bf16[64,768]{1,0:T(8,128)(2,1)S(1)}, u32[]{:S(2)}, u32[]{:S(2)}) collective-permute-start(bf16[64,768]{1,0:T(8,128)(2,1)S(1)} %get-tuple-element.124), channel_id=1, source_target_pairs={{0,3},{1,2},{2,1},{3,0},{4,7},{5,6},{6,5},{7,4},{8,11},{9,10},{10,... | collective-permute-start | bytes 294920 | tf_op jit(solution)/shard_map/ppermute | solution.py:56
  237.0 34.7 %collective-permute-start.34 = (bf16[4,4032,128]{2,1,0:T(8,128)(2,1)}, bf16[4,4032,128]{2,1,0:T(8,128)(2,1)}, u32[]{:S(2)}, u32[]{:S(2)}) collective-permute-start(bf16[4,4032,128]{2,1,0:T(8,128)(2,1)} %get-tuple-element.85), channel_id=1, source_target_pairs={{0,4},{4,0},{8,12},{12,8},{16,20},{20,16},{24,28},{28,24},{1,5},{5... | collective-permute-start | bytes 12386312 | tf_op jit(solution)/shard_map/ppermute | solution.py:56
  238.3 42.4 %collective-permute-start.38 = (bf16[64,768]{1,0:T(8,128)(2,1)}, bf16[64,768]{1,0:T(8,128)(2,1)S(1)}, u32[]{:S(2)}, u32[]{:S(2)}) collective-permute-start(bf16[64,768]{1,0:T(8,128)(2,1)} %multiply_convert_fusion.3), channel_id=1, source_target_pairs={{0,1},{1,0},{2,3},{3,2},{4,5},{5,4},{6,7},{7,6},{8,9},{9,8},{10,11... | collective-permute-start | bytes 294920 | tf_op jit(solution)/shard_map/ppermute | solution.py:56
  240.8 7.2 %collective-permute-start.28 = (bf16[64,768]{1,0:T(8,128)(2,1)S(1)}, bf16[64,768]{1,0:T(8,128)(2,1)S(1)}, u32[]{:S(2)}, u32[]{:S(2)}) collective-permute-start(bf16[64,768]{1,0:T(8,128)(2,1)S(1)} %get-tuple-element.74), channel_id=1, source_target_pairs={{0,1},{1,0},{2,3},{3,2},{4,5},{5,4},{6,7},{7,6},{8,9},{9,8},{10,11... | collective-permute-start | bytes 294920 | tf_op jit(solution)/shard_map/ppermute | solution.py:56
  241.2 6.8 %collective-permute-start.29 = (bf16[64,768]{1,0:T(8,128)(2,1)S(1)}, bf16[64,768]{1,0:T(8,128)(2,1)S(1)}, u32[]{:S(2)}, u32[]{:S(2)}) collective-permute-start(bf16[64,768]{1,0:T(8,128)(2,1)S(1)} %get-tuple-element.74), channel_id=1, source_target_pairs={{0,2},{1,3},{2,0},{3,1},{4,6},{5,7},{6,4},{7,5},{8,10},{9,11},{10,... | collective-permute-start | bytes 294920 | tf_op jit(solution)/shard_map/ppermute | solution.py:56
  243.8 8.4 %collective-permute-start.30 = (bf16[64,768]{1,0:T(8,128)(2,1)S(1)}, bf16[64,768]{1,0:T(8,128)(2,1)S(1)}, u32[]{:S(2)}, u32[]{:S(2)}) collective-permute-start(bf16[64,768]{1,0:T(8,128)(2,1)S(1)} %get-tuple-element.74), channel_id=1, source_target_pairs={{0,3},{1,2},{2,1},{3,0},{4,7},{5,6},{6,5},{7,4},{8,11},{9,10},{10,... | collective-permute-start | bytes 294920 | tf_op jit(solution)/shard_map/ppermute | solution.py:56
  253.7 5.5 %collective-permute-start.31 = (bf16[64,768]{1,0:T(8,128)(2,1)S(1)}, bf16[64,768]{1,0:T(8,128)(2,1)S(1)}, u32[]{:S(2)}, u32[]{:S(2)}) collective-permute-start(bf16[64,768]{1,0:T(8,128)(2,1)S(1)} %get-tuple-element.120), channel_id=1, source_target_pairs={{0,1},{1,0},{2,3},{3,2},{4,5},{5,4},{6,7},{7,6},{8,9},{9,8},{10,11... | collective-permute-start | bytes 294920 | tf_op jit(solution)/shard_map/ppermute | solution.py:56
  255.2 12.1 %collective-permute-start.32 = (bf16[64,768]{1,0:T(8,128)(2,1)S(1)}, bf16[64,768]{1,0:T(8,128)(2,1)S(1)}, u32[]{:S(2)}, u32[]{:S(2)}) collective-permute-start(bf16[64,768]{1,0:T(8,128)(2,1)S(1)} %get-tuple-element.122), channel_id=1, source_target_pairs={{0,2},{1,3},{2,0},{3,1},{4,6},{5,7},{6,4},{7,5},{8,10},{9,11},{10,... | collective-permute-start | bytes 294920 | tf_op jit(solution)/shard_map/ppermute | solution.py:56
  256.2 13.1 %collective-permute-start.33 = (bf16[64,768]{1,0:T(8,128)(2,1)S(1)}, bf16[64,768]{1,0:T(8,128)(2,1)S(1)}, u32[]{:S(2)}, u32[]{:S(2)}) collective-permute-start(bf16[64,768]{1,0:T(8,128)(2,1)S(1)} %get-tuple-element.121), channel_id=1, source_target_pairs={{0,3},{1,2},{2,1},{3,0},{4,7},{5,6},{6,5},{7,4},{8,11},{9,10},{10,... | collective-permute-start | bytes 294920 | tf_op jit(solution)/shard_map/ppermute | solution.py:56
  259.2 22.4 %collective-permute-start.39 = (bf16[64,768]{1,0:T(8,128)(2,1)}, bf16[64,768]{1,0:T(8,128)(2,1)S(1)}, u32[]{:S(2)}, u32[]{:S(2)}) collective-permute-start(bf16[64,768]{1,0:T(8,128)(2,1)} %multiply_convert_fusion.3), channel_id=1, source_target_pairs={{0,2},{1,3},{2,0},{3,1},{4,6},{5,7},{6,4},{7,5},{8,10},{9,11},{10,... | collective-permute-start | bytes 294920 | tf_op jit(solution)/shard_map/ppermute | solution.py:56
  267.3 16.4 %collective-permute-start.40 = (bf16[64,768]{1,0:T(8,128)(2,1)}, bf16[64,768]{1,0:T(8,128)(2,1)S(1)}, u32[]{:S(2)}, u32[]{:S(2)}) collective-permute-start(bf16[64,768]{1,0:T(8,128)(2,1)} %multiply_convert_fusion.3), channel_id=1, source_target_pairs={{0,3},{1,2},{2,1},{3,0},{4,7},{5,6},{6,5},{7,4},{8,11},{9,10},{10,... | collective-permute-start | bytes 294920 | tf_op jit(solution)/shard_map/ppermute | solution.py:56
  269.3 14.9 %collective-permute-start.42 = (bf16[64,128]{1,0:T(8,128)(2,1)S(1)}, bf16[64,128]{1,0:T(8,128)(2,1)S(1)}, u32[]{:S(2)}, u32[]{:S(2)}) collective-permute-start(bf16[64,128]{1,0:T(8,128)(2,1)S(1)} %get-tuple-element.130), channel_id=1, source_target_pairs={{0,2},{1,3},{2,0},{3,1},{4,6},{5,7},{6,4},{7,5},{8,10},{9,11},{10,... | collective-permute-start | bytes 49160 | tf_op jit(solution)/shard_map/ppermute | solution.py:56
  271.8 14.4 %collective-permute-start.43 = (bf16[64,128]{1,0:T(8,128)(2,1)S(1)}, bf16[64,128]{1,0:T(8,128)(2,1)S(1)}, u32[]{:S(2)}, u32[]{:S(2)}) collective-permute-start(bf16[64,128]{1,0:T(8,128)(2,1)S(1)} %get-tuple-element.132), channel_id=1, source_target_pairs={{0,3},{1,2},{2,1},{3,0},{4,7},{5,6},{6,5},{7,4},{8,11},{9,10},{10,... | collective-permute-start | bytes 49160 | tf_op jit(solution)/shard_map/ppermute | solution.py:56
  280.7 5.5 %collective-permute-start.41 = (bf16[64,128]{1,0:T(8,128)(2,1)S(1)}, bf16[64,128]{1,0:T(8,128)(2,1)S(1)}, u32[]{:S(2)}, u32[]{:S(2)}) collective-permute-start(bf16[64,128]{1,0:T(8,128)(2,1)S(1)} %get-tuple-element.131), channel_id=1, source_target_pairs={{0,1},{1,0},{2,3},{3,2},{4,5},{5,4},{6,7},{7,6},{8,9},{9,8},{10,11... | collective-permute-start | bytes 49160 | tf_op jit(solution)/shard_map/ppermute | solution.py:56
  281.6 7.1 %collective-permute-start.35 = (bf16[64,768]{1,0:T(8,128)(2,1)}, bf16[64,768]{1,0:T(8,128)(2,1)}, u32[]{:S(2)}, u32[]{:S(2)}) collective-permute-start(bf16[64,768]{1,0:T(8,128)(2,1)} %get-tuple-element.71), channel_id=1, source_target_pairs={{0,1},{1,0},{2,3},{3,2},{4,5},{5,4},{6,7},{7,6},{8,9},{9,8},{10,11... | collective-permute-start | bytes 294920 | tf_op jit(solution)/shard_map/ppermute | solution.py:56
  283.7 7.9 %collective-permute-start.36 = (bf16[64,768]{1,0:T(8,128)(2,1)}, bf16[64,768]{1,0:T(8,128)(2,1)}, u32[]{:S(2)}, u32[]{:S(2)}) collective-permute-start(bf16[64,768]{1,0:T(8,128)(2,1)} %get-tuple-element.71), channel_id=1, source_target_pairs={{0,2},{1,3},{2,0},{3,1},{4,6},{5,7},{6,4},{7,5},{8,10},{9,11},{10,... | collective-permute-start | bytes 294920 | tf_op jit(solution)/shard_map/ppermute | solution.py:56
  284.2 7.4 %collective-permute-start.37 = (bf16[64,768]{1,0:T(8,128)(2,1)}, bf16[64,768]{1,0:T(8,128)(2,1)}, u32[]{:S(2)}, u32[]{:S(2)}) collective-permute-start(bf16[64,768]{1,0:T(8,128)(2,1)} %get-tuple-element.71), channel_id=1, source_target_pairs={{0,3},{1,2},{2,1},{3,0},{4,7},{5,6},{6,5},{7,4},{8,11},{9,10},{10,... | collective-permute-start | bytes 294920 | tf_op jit(solution)/shard_map/ppermute | solution.py:56
  286.7 27.7 %collective-permute-start.51 = (bf16[2,2016,128]{2,1,0:T(8,128)(2,1)}, bf16[2,2016,128]{2,1,0:T(8,128)(2,1)}, u32[]{:S(2)}, u32[]{:S(2)}) collective-permute-start(bf16[2,2016,128]{2,1,0:T(8,128)(2,1)} %copy-done.34), channel_id=1, source_target_pairs={{0,16},{4,20},{8,24},{12,28},{16,0},{20,4},{24,8},{28,12},{1,17},{... | collective-permute-start | bytes 3096584 | tf_op jit(solution)/shard_map/ppermute | solution.py:56
  287.1 30.9 %collective-permute-start.49 = (bf16[2,2016,128]{2,1,0:T(8,128)(2,1)}, bf16[2,2016,128]{2,1,0:T(8,128)(2,1)}, u32[]{:S(2)}, u32[]{:S(2)}) collective-permute-start(bf16[2,2016,128]{2,1,0:T(8,128)(2,1)} %copy-done.33), channel_id=1, source_target_pairs={{0,8},{4,12},{8,0},{12,4},{16,24},{20,28},{24,16},{28,20},{1,9},{5... | collective-permute-start | bytes 3096584 | tf_op jit(solution)/shard_map/ppermute | solution.py:56
  323.9 7.6 %collective-permute-start.57 = (bf16[64,768]{1,0:T(8,128)(2,1)S(1)}, bf16[64,768]{1,0:T(8,128)(2,1)S(1)}, u32[]{:S(2)}, u32[]{:S(2)}) collective-permute-start(bf16[64,768]{1,0:T(8,128)(2,1)S(1)} %get-tuple-element.119), channel_id=1, source_target_pairs={{0,2},{1,3},{2,0},{3,1},{4,6},{5,7},{6,4},{7,5},{8,10},{9,11},{10,... | collective-permute-start | bytes 294920 | tf_op jit(solution)/shard_map/ppermute | solution.py:56
  324.7 6.8 %collective-permute-start.58 = (bf16[64,768]{1,0:T(8,128)(2,1)S(1)}, bf16[64,768]{1,0:T(8,128)(2,1)S(1)}, u32[]{:S(2)}, u32[]{:S(2)}) collective-permute-start(bf16[64,768]{1,0:T(8,128)(2,1)S(1)} %get-tuple-element.118), channel_id=1, source_target_pairs={{0,3},{1,2},{2,1},{3,0},{4,7},{5,6},{6,5},{7,4},{8,11},{9,10},{10,... | collective-permute-start | bytes 294920 | tf_op jit(solution)/shard_map/ppermute | solution.py:56
  326.9 48.3 %collective-permute-start.44 = (bf16[4,304,768]{2,1,0:T(8,128)(2,1)S(1)}, bf16[4,304,768]{2,1,0:T(8,128)(2,1)S(1)}, u32[]{:S(2)}, u32[]{:S(2)}) collective-permute-start(bf16[4,304,768]{2,1,0:T(8,128)(2,1)S(1)} %get-tuple-element.91), channel_id=1, source_target_pairs={{0,4},{4,0},{8,12},{12,8},{16,20},{20,16},{24,28},{28,24},{1,5},{5... | collective-permute-start | bytes 5603336 | tf_op jit(solution)/shard_map/ppermute | solution.py:56
  332.0 30.8 %collective-permute-start.50 = (bf16[2016,128]{1,0:T(8,128)(2,1)S(1)}, bf16[2016,128]{1,0:T(8,128)(2,1)S(1)}, u32[]{:S(2)}, u32[]{:S(2)}) collective-permute-start(bf16[2016,128]{1,0:T(8,128)(2,1)S(1)} %fusion.35), channel_id=1, source_target_pairs={{0,16},{4,20},{8,24},{12,28},{16,0},{20,4},{24,8},{28,12},{1,17},{... | collective-permute-start | bytes 1548296 | tf_op jit(solution)/shard_map/ppermute | solution.py:56
  336.9 9.7 %collective-permute-start.68 = (f32[34,128]{1,0:T(8,128)S(1)}, f32[34,128]{1,0:T(8,128)S(1)}, u32[]{:S(2)}, u32[]{:S(2)}) collective-permute-start(f32[34,128]{1,0:T(8,128)S(1)} %fusion.179), channel_id=1, source_target_pairs={{0,16},{4,20},{8,24},{12,28},{16,0},{20,4},{24,8},{28,12},{1,17},{... | collective-permute-start | bytes 52232 | tf_op jit(solution)/shard_map/ppermute | solution.py:56
  349.0 5.6 %collective-permute-start.71 = (f32[34,128]{1,0:T(8,128)S(1)}, f32[34,128]{1,0:T(8,128)S(1)}, u32[]{:S(2)}, u32[]{:S(2)}) collective-permute-start(f32[34,128]{1,0:T(8,128)S(1)} %add.530), channel_id=1, source_target_pairs={{0,3},{1,2},{2,1},{3,0},{4,7},{5,6},{6,5},{7,4},{8,11},{9,10},{10,... | collective-permute-start | bytes 52232 | tf_op jit(solution)/shard_map/ppermute | solution.py:56
  351.1 6.2 %collective-permute-start.59 = (bf16[64,768]{1,0:T(8,128)(2,1)S(1)}, bf16[64,768]{1,0:T(8,128)(2,1)S(1)}, u32[]{:S(2)}, u32[]{:S(2)}) collective-permute-start(bf16[64,768]{1,0:T(8,128)(2,1)S(1)} %add_convert_fusion.4), channel_id=1, source_target_pairs={{0,1},{1,0},{2,3},{3,2},{4,5},{5,4},{6,7},{7,6},{8,9},{9,8},{10,11... | collective-permute-start | bytes 294920 | tf_op jit(solution)/shard_map/ppermute | solution.py:56
  353.2 8.9 %collective-permute-start.60 = (bf16[64,768]{1,0:T(8,128)(2,1)S(1)}, bf16[64,768]{1,0:T(8,128)(2,1)S(1)}, u32[]{:S(2)}, u32[]{:S(2)}) collective-permute-start(bf16[64,768]{1,0:T(8,128)(2,1)S(1)} %add_convert_fusion.4), channel_id=1, source_target_pairs={{0,2},{1,3},{2,0},{3,1},{4,6},{5,7},{6,4},{7,5},{8,10},{9,11},{10,... | collective-permute-start | bytes 294920 | tf_op jit(solution)/shard_map/ppermute | solution.py:56
  354.6 7.5 %collective-permute-start.61 = (bf16[64,768]{1,0:T(8,128)(2,1)S(1)}, bf16[64,768]{1,0:T(8,128)(2,1)S(1)}, u32[]{:S(2)}, u32[]{:S(2)}) collective-permute-start(bf16[64,768]{1,0:T(8,128)(2,1)S(1)} %add_convert_fusion.4), channel_id=1, source_target_pairs={{0,3},{1,2},{2,1},{3,0},{4,7},{5,6},{6,5},{7,4},{8,11},{9,10},{10,... | collective-permute-start | bytes 294920 | tf_op jit(solution)/shard_map/ppermute | solution.py:56
  357.3 11.5 %collective-permute-start.52 = (bf16[2016,128]{1,0:T(8,128)(2,1)S(1)}, bf16[2016,128]{1,0:T(8,128)(2,1)S(1)}, u32[]{:S(2)}, u32[]{:S(2)}) collective-permute-start(bf16[2016,128]{1,0:T(8,128)(2,1)S(1)} %fusion.36), channel_id=1, source_target_pairs={{0,8},{4,12},{8,0},{12,4},{16,24},{20,28},{24,16},{28,20},{1,9},{5... | collective-permute-start | bytes 1548296 | tf_op jit(solution)/shard_map/ppermute | solution.py:56
  362.7 9.8 %collective-permute-start.62 = (f32[168,768]{1,0:T(8,128)S(1)}, f32[168,768]{1,0:T(8,128)S(1)}, u32[]{:S(2)}, u32[]{:S(2)}) collective-permute-start(f32[168,768]{1,0:T(8,128)S(1)} %pad_select_fusion), channel_id=1, source_target_pairs={{0,4},{4,0},{8,12},{12,8},{16,20},{20,16},{24,28},{28,24},{1,5},{5... | collective-permute-start | bytes 1548296 | tf_op jit(solution)/shard_map/ppermute | solution.py:56
  370.0 19.6 %collective-permute-start.53 = (bf16[1008,128]{1,0:T(8,128)(2,1)}, bf16[1008,128]{1,0:T(8,128)(2,1)}, u32[]{:S(2)}, u32[]{:S(2)}) collective-permute-start(bf16[1008,128]{1,0:T(8,128)(2,1)} %get-tuple-element.92), channel_id=1, source_target_pairs={{0,1},{1,0},{2,3},{3,2},{4,5},{5,4},{6,7},{7,6},{8,9},{9,8},{10,11... | collective-permute-start | bytes 774152 | tf_op jit(solution)/shard_map/ppermute | solution.py:56
  370.0 19.9 %collective-permute-start.54 = (bf16[1008,128]{1,0:T(8,128)(2,1)}, bf16[1008,128]{1,0:T(8,128)(2,1)}, u32[]{:S(2)}, u32[]{:S(2)}) collective-permute-start(bf16[1008,128]{1,0:T(8,128)(2,1)} %get-tuple-element.94), channel_id=1, source_target_pairs={{0,2},{1,3},{2,0},{3,1},{4,6},{5,7},{6,4},{7,5},{8,10},{9,11},{10,... | collective-permute-start | bytes 774152 | tf_op jit(solution)/shard_map/ppermute | solution.py:56
  372.5 8.2 %collective-permute-start.63 = (bf16[168,768]{1,0:T(8,128)(2,1)S(1)}, bf16[168,768]{1,0:T(8,128)(2,1)S(1)}, u32[]{:S(2)}, u32[]{:S(2)}) collective-permute-start(bf16[168,768]{1,0:T(8,128)(2,1)S(1)} %fusion.142), channel_id=1, source_target_pairs={{8,0},{9,1},{10,2},{11,3},{12,4}} | collective-permute-start | bytes 774152 | tf_op jit(solution)/shard_map/ppermute | solution.py:151
  373.8 12.9 %collective-permute-start.64 = (bf16[168,768]{1,0:T(8,128)(2,1)S(1)}, bf16[168,768]{1,0:T(8,128)(2,1)S(1)}, u32[]{:S(2)}, u32[]{:S(2)}) collective-permute-start(bf16[168,768]{1,0:T(8,128)(2,1)S(1)} %fusion.142), channel_id=1, source_target_pairs={{16,0},{17,1},{18,2},{19,3},{20,4}} | collective-permute-start | bytes 774152 | tf_op jit(solution)/shard_map/ppermute | solution.py:151
  375.2 11.6 %collective-permute-start.65 = (bf16[168,768]{1,0:T(8,128)(2,1)S(1)}, bf16[168,768]{1,0:T(8,128)(2,1)S(1)}, u32[]{:S(2)}, u32[]{:S(2)}) collective-permute-start(bf16[168,768]{1,0:T(8,128)(2,1)S(1)} %fusion.142), channel_id=1, source_target_pairs={{24,0},{25,1},{26,2},{27,3},{28,4}} | collective-permute-start | bytes 774152 | tf_op jit(solution)/shard_map/ppermute | solution.py:151
  380.8 9.1 %collective-permute-start.55 = (bf16[1008,128]{1,0:T(8,128)(2,1)}, bf16[1008,128]{1,0:T(8,128)(2,1)}, u32[]{:S(2)}, u32[]{:S(2)}) collective-permute-start(bf16[1008,128]{1,0:T(8,128)(2,1)} %get-tuple-element.93), channel_id=1, source_target_pairs={{0,3},{1,2},{2,1},{3,0},{4,7},{5,6},{6,5},{7,4},{8,11},{9,10},{10,... | collective-permute-start | bytes 774152 | tf_op jit(solution)/shard_map/ppermute | solution.py:56
  386.7 9.1 %collective-permute-start.45 = (bf16[2,152,768]{2,1,0:T(8,128)(2,1)}, bf16[2,152,768]{2,1,0:T(8,128)(2,1)}, u32[]{:S(2)}, u32[]{:S(2)}) collective-permute-start(bf16[2,152,768]{2,1,0:T(8,128)(2,1)} %fusion.40), channel_id=1, source_target_pairs={{0,8},{4,12},{8,0},{12,4},{16,24},{20,28},{24,16},{28,20},{1,9},{5... | collective-permute-start | bytes 1400840 | tf_op jit(solution)/shard_map/ppermute | solution.py:56
  386.7 11.7 %collective-permute-start.47 = (bf16[2,152,768]{2,1,0:T(8,128)(2,1)}, bf16[2,152,768]{2,1,0:T(8,128)(2,1)}, u32[]{:S(2)}, u32[]{:S(2)}) collective-permute-start(bf16[2,152,768]{2,1,0:T(8,128)(2,1)} %fusion.41), channel_id=1, source_target_pairs={{0,16},{4,20},{8,24},{12,28},{16,0},{20,4},{24,8},{28,12},{1,17},{... | collective-permute-start | bytes 1400840 | tf_op jit(solution)/shard_map/ppermute | solution.py:56
  397.2 6.1 %collective-permute-start.46 = (bf16[152,768]{1,0:T(8,128)(2,1)S(1)}, bf16[152,768]{1,0:T(8,128)(2,1)S(1)}, u32[]{:S(2)}, u32[]{:S(2)}) collective-permute-start(bf16[152,768]{1,0:T(8,128)(2,1)S(1)} %fusion.63), channel_id=1, source_target_pairs={{0,16},{4,20},{8,24},{12,28},{16,0},{20,4},{24,8},{28,12},{1,17},{... | collective-permute-start | bytes 700424 | tf_op jit(solution)/shard_map/ppermute | solution.py:56
  399.7 6.1 %collective-permute-start.48 = (bf16[152,768]{1,0:T(8,128)(2,1)S(1)}, bf16[152,768]{1,0:T(8,128)(2,1)S(1)}, u32[]{:S(2)}, u32[]{:S(2)}) collective-permute-start(bf16[152,768]{1,0:T(8,128)(2,1)S(1)} %fusion.64), channel_id=1, source_target_pairs={{0,8},{4,12},{8,0},{12,4},{16,24},{20,28},{24,16},{28,20},{1,9},{5... | collective-permute-start | bytes 700424 | tf_op jit(solution)/shard_map/ppermute | solution.py:56
  (92 other events, 618.4 us)
Sparse Core Ops, SparseCore 0:
  10.5 39.7 all-gather.3
  55.9 57.4 all-gather.5
